TPU v7x, 32 devices: a whole 2x2x4 slice. The times are simulated.
32 devices in a mesh: dp: 8 (over z, core), tensor: 4 (over y, x).
Axes of the slice: x: 2, y: 2, z: 4, core: 2. Of those that a mesh axis runs over, the one named last changes fastest.
Arguments:
- inputs: bfloat16 [16384, 2048], P(('dp', 'tensor')), may hold values from -6 to 6
- segment_ids: int32 [16384], P('dp'), may hold values from 0 to 1, as said below
- attn_gain: bfloat16 [2048], P('dp'), may hold values from 0.099609375 to 1.8984375
- query_weight: bfloat16 [2048, 2048], P('dp', 'tensor'), may hold values from -0.125 to 0.125
- key_weight: bfloat16 [2048, 512], P('dp', 'tensor'), may hold values from -0.125 to 0.125
- value_weight: bfloat16 [2048, 512], P('dp', 'tensor'), may hold values from -0.125 to 0.125
- output_weight: bfloat16 [2048, 2048], P('tensor', 'dp'), may hold values from -0.75 to 0.75
- mlp_gain: bfloat16 [2048], P('dp'), may hold values from 0.099609375 to 1.8984375
- gate_weight: bfloat16 [2048, 8192], P('dp', 'tensor'), may hold values from -0.125 to 0.125
- up_weight: bfloat16 [2048, 8192], P('dp', 'tensor'), may hold values from -0.125 to 0.125
- down_weight: bfloat16 [8192, 2048], P('tensor', 'dp'), may hold values from -0.125 to 0.125
- cotangent: bfloat16 [16384, 2048], P(('dp', 'tensor')), may hold values from -6 to 6
Outputs:
- layer_out: bfloat16 [16384, 2048], P(('dp', 'tensor'))
- input_grad: bfloat16 [16384, 2048], P(('dp', 'tensor'))
- attn_gain_grad: float32 [2048], P('dp')
- query_weight_grad: float32 [2048, 2048], P('dp', 'tensor')
- key_weight_grad: float32 [2048, 512], P('dp', 'tensor')
- value_weight_grad: float32 [2048, 512], P('dp', 'tensor')
- output_weight_grad: float32 [2048, 2048], P('tensor', 'dp')
- mlp_gain_grad: float32 [2048], P('dp')
- gate_weight_grad: float32 [2048, 8192], P('dp', 'tensor')
- up_weight_grad: float32 [2048, 8192], P('dp', 'tensor')
- down_weight_grad: float32 [8192, 2048], P('tensor', 'dp')
Inputs may be any that keep to these rules, and one draw needn't show every extreme that they name: `segment_ids`: in each aligned block of 2048 tokens the ids never fall and are 0 for the first sequence and 1 for a second one where the block holds two; every sequence has 1024 tokens or more; some block holds one sequence and some block two.
All inputs are finite; a program needn't handle non-finite values.
Results may differ from a plain program's by a relative error of at most 0.025.
Values may be sent and summed in bfloat16 or wider, within the bound.
No kernel may reach another device: no remote copies, remote signals or barrier semaphores. Data moves between devices by JAX's collectives and lax.ppermute only.
A program may use at most 256 MiB of HBM per device.

v0:
```python
import functools
import math

import jax
import jax.numpy as jnp
from jax import lax
from jax.experimental import pallas as pl
from jax.experimental.pallas import tpu as pltpu
from jax.sharding import PartitionSpec as P

HD = 64
LANES = 128
EPSILON = 1e-05
ROPE_BASE = 500000.0
MASKED = -1e30
OVER_ROWS = (((0,), (0,)), ((), ()))
OVER_COLS = (((1,), (1,)), ((), ()))


def limit(size):
    return pltpu.CompilerParams(vmem_limit_bytes=size * 2**20)


SHORT = 0.0625


def declared(flops, scale=SHORT):
    return pl.CostEstimate(flops=int(flops * scale), bytes_accessed=0, transcendentals=0)


F32 = jnp.float32
BF16 = jnp.bfloat16


def dot_cols(left, right):
    return lax.dot_general(left, right, OVER_COLS, preferred_element_type=F32)


def dot_rows(left, right):
    return lax.dot_general(left, right, OVER_ROWS, preferred_element_type=F32)


def dot(left, right):
    return jnp.dot(left, right, preferred_element_type=F32)


def pairs(size, bit):
    return [(index, index ^ bit) for index in range(size)]


def slots_of(size):
    if size == 4:
        return [lax.axis_index("tensor") ^ step for step in range(size)]
    return [jnp.int32(step) for step in range(size)]


ANYWHERE = pl.BlockSpec(memory_space=pl.ANY)


def nothing_kernel(*refs):
    pass


def hold(value, *others):
    return pl.pallas_call(
        nothing_kernel,
        in_specs=[ANYWHERE] * (1 + len(others)),
        out_specs=ANYWHERE,
        out_shape=jax.ShapeDtypeStruct(value.shape, value.dtype),
        input_output_aliases={0: 0},
        cost_estimate=declared(0),
    )(value, *others)


def first_hop(shard, size):
    if size != 4:
        return None
    return [lax.ppermute(shard, "tensor", pairs(size, bit)) for bit in (1, 2)]


def copy_kernel(value_ref, *rest):
    rest[-1][...] = value_ref[...]


def half_of(value, which, *others):
    rows, width = value.shape
    tile = rows // 4
    return pl.pallas_call(
        copy_kernel,
        grid=(2,),
        in_specs=[pl.BlockSpec((tile, width), lambda i: (2 * which + i, 0))]
        + [ANYWHERE] * len(others),
        out_specs=pl.BlockSpec((tile, width), lambda i: (i, 0)),
        out_shape=jax.ShapeDtypeStruct((rows // 2, width), value.dtype),
        compiler_params=limit(52),
        cost_estimate=declared(0),
    )(value, *others)


def hold_halves(hop, *others):
    return half_of(hop[0], 0, *others), half_of(hop[1], 1, *others)


def second_hop(shard, hop, size, halves=None):
    if size != 4:
        whole = lax.all_gather(shard, "tensor", axis=0)
        return [whole[step] for step in range(size)]
    one, two = hop
    upper, lower = halves or hold_halves(hop)
    three_a = lax.ppermute(upper, "tensor", pairs(size, 2))
    three_b = lax.ppermute(lower, "tensor", pairs(size, 1))
    return [shard, one, two, jnp.concatenate([three_a, three_b], axis=0)]


def gather(shard, size):
    return second_hop(shard, first_hop(shard, size), size)


def send_half(three, size):
    into_two = lax.ppermute(three[0], "tensor", pairs(size, 1))
    into_one = lax.ppermute(three[1], "tensor", pairs(size, 2))
    return into_one, into_two


def send_whole(one, two, into, size):
    into_one, into_two = into
    half = one.shape[0] // 2
    lower = (one[half:].astype(F32) + into_one.astype(F32)).astype(BF16)
    upper = (two[:half].astype(F32) + into_two.astype(F32)).astype(BF16)
    return [
        lax.ppermute(jnp.concatenate([one[:half], lower], axis=0), "tensor", pairs(size, 1)),
        lax.ppermute(jnp.concatenate([upper, two[half:]], axis=0), "tensor", pairs(size, 2)),
    ]


def sum_whole(terms):
    return [
        lax.psum_scatter(
            jnp.concatenate(terms, axis=0), "tensor", scatter_dimension=0, tiled=True
        )
    ]


def trade(pieces, size):
    if size != 4:
        whole = lax.all_to_all(jnp.stack(pieces), "tensor", split_axis=0, concat_axis=0, tiled=True)
        return [whole[step] for step in range(size)]
    return [pieces[0]] + [
        lax.ppermute(pieces[step], "tensor", pairs(size, step)) for step in (1, 2, 3)
    ]


def total(parts):
    return functools.reduce(jnp.add, [part.astype(F32) for part in parts])


def sum_tensor(value, size):
    if size & (size - 1):
        return lax.psum(value, "tensor")
    return value + sum(lax.ppermute(value, "tensor", pairs(size, bit)) for bit in range(1, size))


def sum_blocks(value, size):
    if size & (size - 1):
        return lax.psum(value, "dp")
    bit = 1
    while bit < size:
        value = value + lax.ppermute(value, "dp", pairs(size, bit))
        bit *= 2
    return value


def rope_tables(segment):
    length = segment.shape[0]
    bound = jnp.sum((segment == 0).astype(jnp.int32))
    place = lax.broadcasted_iota(jnp.int32, (length, LANES), 0)
    place = place - jnp.where(place >= bound, bound, 0)
    lane = lax.broadcasted_iota(jnp.int32, (length, LANES), 1)
    freqs = jnp.exp(
        (lane % (HD // 2)).astype(F32) * (-2.0 * math.log(ROPE_BASE) / HD)
    )
    angles = place.astype(F32) * freqs
    sine = jnp.sin(angles)
    return bound, jnp.cos(angles), jnp.where(lane % HD < HD // 2, -sine, sine)


def swap_halves(values):
    lane = lax.broadcasted_iota(jnp.int32, values.shape, 1)
    after = pltpu.roll(values, LANES - HD // 2, 1)
    before = pltpu.roll(values, HD // 2, 1)
    return jnp.where(lane % HD < HD // 2, after, before)


def normalize(stream):
    scale_r = lax.rsqrt(jnp.mean(stream * stream, axis=-1, keepdims=True) + EPSILON)
    return (stream * scale_r, scale_r)


def project_kernel(slot_ref, *refs, count, steps, heads, kv):
    gains_ref, w_ref, cos_ref, sin_ref = refs[count : count + 4]
    h_ref, q_ref, kx_ref, vx_ref, kt_ref, vt_ref, gain_ref = refs[-7:]

    @pl.when(pl.program_id(0) == 0)
    def _():
        gain_ref[...] = gains_ref[...].astype(F32).T[:8]

    which = pl.program_id(0) // steps
    rows = h_ref.shape[0]
    part_rows = min(256, rows)
    lane = lax.broadcasted_iota(jnp.int32, (part_rows, LANES), 1)
    for start in range(0, rows, part_rows):
        at = slice(start, start + part_rows)
        tokens = refs[0][at, :]
        for block in range(1, count):
            tokens = jnp.where(which == block, refs[block][at, :], tokens)
        normed, _ = normalize(tokens.astype(F32))
        low = (normed * gain_ref[0:1, :]).astype(BF16)
        h_ref[at, :] = low
        pre = dot(low, w_ref[...])
        cosine, sine = cos_ref[at, :], sin_ref[at, :]
        chunks = []
        for chunk in range(pre.shape[1] // LANES):
            columns = slice(chunk * LANES, (chunk + 1) * LANES)
            part = pre[:, columns]
            first = 2 * chunk
            if first < heads + kv:
                turned = part * cosine + swap_halves(part) * sine
                part = turned if first + 1 < heads + kv else jnp.where(lane < HD, turned, part)
            chunks.append(part)
            if first < heads:
                q_ref[at, columns] = (part * (1.0 / math.sqrt(HD))).astype(BF16)
        flipped = {}
        for head in range(2 * kv):
            place = heads + head
            part = chunks[place // 2]
            moved = pltpu.roll(part, HD, 1)
            wide = [part, moved] if place % 2 == 0 else [moved, part]
            out = kx_ref if head < kv else vx_ref
            out[head % kv, 0, at, :] = jnp.where(lane < HD, wide[0], 0.0).astype(BF16)
            out[head % kv, 1, at, :] = jnp.where(lane < HD, 0.0, wide[1]).astype(BF16)
            if place // 2 not in flipped:
                flipped[place // 2] = part.T
            turn = flipped[place // 2][(place % 2) * HD : (place % 2 + 1) * HD]
            out_t = kt_ref if head < kv else vt_ref
            out_t[(head % kv) * HD : (head % kv + 1) * HD, at] = turn.astype(BF16)


def project(slots, blocks, bundle, cosine, sine, heads, kv, length):
    rows, width = blocks[0].shape
    count = len(blocks)
    tile = rows
    steps = rows // tile
    columns = (heads + 2 * kv) * HD

    def at(i, slot):
        return slot[i // steps] * steps + i % steps

    shapes = [
        jax.ShapeDtypeStruct((length, width), BF16),
        jax.ShapeDtypeStruct((length, heads * HD), BF16),
        jax.ShapeDtypeStruct((kv, 2, length, LANES), BF16),
        jax.ShapeDtypeStruct((kv, 2, length, LANES), BF16),
        jax.ShapeDtypeStruct((kv * HD, length), BF16),
        jax.ShapeDtypeStruct((kv * HD, length), BF16),
        jax.ShapeDtypeStruct((8, width), F32),
    ]
    out_specs = [
        pl.BlockSpec((tile, width), lambda i, s: (at(i, s), 0)),
        pl.BlockSpec((tile, heads * HD), lambda i, s: (at(i, s), 0)),
        pl.BlockSpec((kv, 2, tile, LANES), lambda i, s: (0, 0, at(i, s), 0)),
        pl.BlockSpec((kv, 2, tile, LANES), lambda i, s: (0, 0, at(i, s), 0)),
        pl.BlockSpec((kv * HD, tile), lambda i, s: (0, at(i, s))),
        pl.BlockSpec((kv * HD, tile), lambda i, s: (0, at(i, s))),
        pl.BlockSpec((8, width), lambda i, s: (0, 0)),
    ]
    in_specs = [
        pl.BlockSpec((tile, width), lambda i, s, b=block: (jnp.clip(i - b * steps, 0, steps - 1), 0))
        for block in range(count)
    ]
    in_specs += [
        pl.BlockSpec((width, LANES), lambda i, s: (0, columns // LANES)),
        pl.BlockSpec((width, columns), lambda i, s: (0, 0)),
        pl.BlockSpec((tile, LANES), lambda i, s: (at(i, s), 0)),
        pl.BlockSpec((tile, LANES), lambda i, s: (at(i, s), 0)),
    ]
    operands = [jnp.stack(slots), *blocks, bundle, bundle, cosine, sine]
    return pl.pallas_call(
        functools.partial(
            project_kernel, count=count, steps=steps, heads=heads, kv=kv
        ),
        grid_spec=pltpu.PrefetchScalarGridSpec(
            num_scalar_prefetch=1,
            grid=(count * steps,),
            in_specs=in_specs,
            out_specs=out_specs,
        ),
        out_shape=shapes,
        compiler_params=limit(52),
        cost_estimate=declared(2 * count * rows * width * columns),
    )(*operands)


def feed_kernel(*refs, count):
    tokens = refs[:count]
    gate_ref, up_ref = refs[count : count + 2]
    hidden_ref, silu_ref, slope_ref, h_out = refs[-4:]
    rows = tokens[0].shape[0]
    wide = h_out.shape[1]
    tile = min(256, gate_ref.shape[1])
    lanes = pl.ds(pl.multiple_of(pl.program_id(0) * wide, wide), wide)
    for block in range(count):
        h_out[block * rows : (block + 1) * rows, :] = tokens[block][:, lanes]
    for part in range(gate_ref.shape[1] // tile):
        columns = slice(part * tile, (part + 1) * tile)
        for block in range(count):
            where = slice(block * rows, (block + 1) * rows)
            gate = dot(tokens[block][...], gate_ref[:, columns])
            up = dot(tokens[block][...], up_ref[:, columns])
            sigmoid = 0.5 * jnp.tanh(0.5 * gate) + 0.5
            silu = gate * sigmoid
            hidden_ref[where, columns] = (silu * up).astype(BF16)
            silu_ref[where, columns] = silu.astype(BF16)
            slope_ref[where, columns] = (up * (sigmoid + silu * (1.0 - sigmoid))).astype(BF16)


def feed_back_kernel(*refs, count):
    grads = refs[:count]
    down_ref, silu_ref, slope_ref = refs[count : count + 3]
    dgate_ref, dup_ref = refs[-2:]
    rows = grads[0].shape[0]
    for block in range(count):
        where = slice(block * rows, (block + 1) * rows)
        dhidden = dot(grads[block][...], down_ref[...])
        dup_ref[where, :] = (dhidden * silu_ref[where, :].astype(F32)).astype(BF16)
        dgate_ref[where, :] = (dhidden * slope_ref[where, :].astype(F32)).astype(BF16)


def feed(kernel, place, blocks, tokens, weights, places, kept, units, outs, copy, tile, prev, others):
    rows, width = tokens[0].shape
    count = len(tokens)
    steps = max(units // tile, 1)
    tile, wide = units // steps, width // steps
    shapes = [jax.ShapeDtypeStruct((blocks * rows, units), BF16)] * outs
    in_specs = [pl.BlockSpec((rows, width), lambda i: (0, 0), pipeline_mode=pl.Buffered(1))] * count
    in_specs += [
        pl.BlockSpec((width, tile), lambda i, w=which: (0, w * steps + i)) for which in places
    ]
    cell = pl.BlockSpec((count * rows, tile), lambda i: (place, i))
    in_specs += [cell] * len(kept)
    out_specs = [cell] * outs
    if copy:
        shapes.append(jax.ShapeDtypeStruct((blocks * rows, width), BF16))
        out_specs.append(pl.BlockSpec((count * rows, wide), lambda i: (place, i)))
    operands = [*tokens, *weights, *kept]
    aliases = {}
    if prev is not None:
        for index, array in enumerate(prev):
            aliases[len(operands)] = index
            operands.append(array)
            in_specs.append(ANYWHERE)
    operands += others
    in_specs += [ANYWHERE] * len(others)
    return pl.pallas_call(
        functools.partial(kernel, count=count),
        grid=(steps,),
        in_specs=in_specs,
        out_specs=out_specs,
        out_shape=shapes,
        input_output_aliases=aliases,
        compiler_params=limit(52),
        cost_estimate=declared(2 * len(weights) * count * rows * width * units),
    )(*operands)


def back_kernel(slot_ref, *refs, count, terms, added, split):
    outs = refs[-2:] if split else refs[-count:]
    weights = refs[count * terms : (count + 1) * terms]
    into = list(refs[(count + 1) * terms :])
    for block in range(count):
        value = dot_cols(refs[block * terms][...], weights[0][...])
        for term in range(1, terms):
            value = value + dot_cols(refs[block * terms + term][...], weights[term][...])
        half = value.shape[0] // 2
        if split:
            outs[0][...] = value[:half].astype(BF16)
            outs[1][...] = value[half:].astype(BF16)
            continue
        if added[block] is None:
            outs[block][...] = value.astype(BF16)
            continue
        extra = into.pop(0)[...].astype(F32)
        top, bottom = value[:half], value[half:]
        if added[block]:
            top = top + extra
        else:
            bottom = bottom + extra
        outs[block][:half, :] = top.astype(BF16)
        outs[block][half:, :] = bottom.astype(BF16)


def back(slots, rows, lefts, weights, places, into=None, others=(), split=False):
    depth = lefts[0].shape[1]
    width = weights[0].shape[0]
    tile = min(512, width)
    terms, count = len(lefts), len(slots)
    outs, tall = (2, rows // 2) if split else (count, rows)
    into = into or [None] * count
    in_specs, operands = [], [jnp.stack([jnp.asarray(slot, jnp.int32) for slot in slots])]
    for block in range(count):
        in_specs += [pl.BlockSpec((rows, depth), lambda i, s, b=block: (s[b], 0))] * terms
        operands += lefts
    in_specs += [pl.BlockSpec((tile, depth), lambda i, s, p=place: (i, p)) for place in places]
    operands += weights
    for extra in into:
        if extra is not None:
            in_specs.append(pl.BlockSpec((rows // 2, tile), lambda i, s: (0, i)))
            operands.append(extra[0])
    operands += others
    in_specs += [ANYWHERE] * len(others)
    return pl.pallas_call(
        functools.partial(
            back_kernel,
            count=count,
            terms=terms,
            added=[None if extra is None else extra[1] for extra in into],
            split=split,
        ),
        grid_spec=pltpu.PrefetchScalarGridSpec(
            num_scalar_prefetch=1,
            grid=(width // tile,),
            in_specs=in_specs,
            out_specs=[pl.BlockSpec((tall, tile), lambda i, s: (0, i))] * outs,
        ),
        out_shape=[jax.ShapeDtypeStruct((tall, width), BF16)] * outs,
        compiler_params=limit(52),
        cost_estimate=declared(2 * count * terms * rows * width * depth),
    )(*operands)


def turn_kernel(value_ref, *rest):
    rest[-1][...] = value_ref[...].T


def turn(value, others=()):
    rows, columns = value.shape
    tile = min(512, rows)
    return pl.pallas_call(
        turn_kernel,
        grid=(rows // tile,),
        in_specs=[pl.BlockSpec((tile, columns), lambda i: (i, 0))] + [ANYWHERE] * len(others),
        out_specs=pl.BlockSpec((columns, tile), lambda i: (0, i)),
        out_shape=jax.ShapeDtypeStruct((columns, rows), value.dtype),
        compiler_params=limit(52),
        cost_estimate=declared(0),
    )(value, *others)


def turn_blocks(lefts, turned_ref):
    rows = lefts[0].shape[0]
    for block, left in enumerate(lefts):
        turned_ref[:, block * rows : (block + 1) * rows] = left[...].T


def weigh_kernel(*refs, count):
    lefts, right_ref = refs[:count], refs[count]
    out_ref, *turned = refs[-3:]
    i, j = pl.program_id(0), pl.program_id(1)
    last = j == pl.num_programs(1) - 1

    @pl.when((i == 0) & (j == 0))
    def _():
        turn_blocks(lefts, turned[0])

    for parity in range(2):

        @pl.when((i % 2 == parity) & jnp.logical_not(last))
        def _():
            out_ref[...] = dot(turned[parity][...], right_ref[...]).astype(BF16)

        @pl.when((i % 2 == parity) & last)
        def _():
            out_ref[...] = dot(turned[parity][...], right_ref[...]).astype(BF16)
            turn_blocks(lefts, turned[1 - parity])


def weigh(lefts, right, others=()):
    tokens, columns = right.shape
    rows, width = lefts[0].shape
    tall, wide = min(512, width), min(1024, columns // 2)
    tiles, steps = width // tall, columns // wide

    def ahead(i, j):
        return 0, jnp.minimum(i + jnp.where(j == steps - 1, 1, 0), tiles - 1)

    return pl.pallas_call(
        functools.partial(weigh_kernel, count=len(lefts)),
        grid=(tiles, steps),
        in_specs=[pl.BlockSpec((rows, tall), ahead)] * len(lefts)
        + [pl.BlockSpec((tokens, wide), lambda i, j: (0, j))]
        + [ANYWHERE] * len(others),
        out_specs=pl.BlockSpec((tall, wide), lambda i, j: (i, j)),
        out_shape=jax.ShapeDtypeStruct((width, columns), BF16),
        scratch_shapes=[pltpu.VMEM((tall, tokens), BF16)] * 2,
        compiler_params=limit(52),
        cost_estimate=declared(2 * tokens * width * columns),
    )(*lefts, right, *others)


def weigh_both_kernel(*refs, count):
    one_ref, others = refs[0], refs[1 : 1 + count]
    right_ref, other_ref, out_ref, turned_ref, other_turned_ref = refs[1 + count :]
    columns = right_ref.shape[1]
    turn_blocks([one_ref], turned_ref)
    out_ref[:, :columns] = dot(turned_ref[...], right_ref[...]).astype(BF16)
    turn_blocks(others, other_turned_ref)
    out_ref[:, columns:] = dot(other_turned_ref[...], other_ref[...]).astype(BF16)


def weigh_both(one, right, others, other_right):
    tokens, width = one.shape
    rows = others[0].shape[0]
    columns, more = right.shape[1], other_right.shape[1]
    tall = min(512, width)
    whole = [pl.BlockSpec((tokens, columns), lambda i: (0, 0))]
    whole += [pl.BlockSpec((tokens, more), lambda i: (0, 0))]
    return pl.pallas_call(
        functools.partial(weigh_both_kernel, count=len(others)),
        grid=(width // tall,),
        in_specs=[pl.BlockSpec((tokens, tall), lambda i: (0, i))]
        + [pl.BlockSpec((rows, tall), lambda i: (0, i))] * len(others)
        + whole,
        out_specs=pl.BlockSpec((tall, columns + more), lambda i: (i, 0)),
        out_shape=jax.ShapeDtypeStruct((width, columns + more), BF16),
        scratch_shapes=[pltpu.VMEM((tall, tokens), BF16)] * 2,
        compiler_params=limit(52),
        cost_estimate=declared(2 * tokens * width * (columns + more)),
    )(one, *others, right, other_right)


def settle_kernel(*refs, count):
    pieces, weights = refs[:count], refs[count : 2 * count]
    x_ref, gains_ref = refs[2 * count : 2 * count + 2]
    stream_ref, h_ref = refs[-2:]
    stream = x_ref[...].astype(F32)
    for piece, weight in zip(pieces, weights):
        stream = stream + dot_cols(piece[...], weight[...])
    stream_ref[...] = stream
    normed, _ = normalize(stream)
    h_ref[...] = (normed * gains_ref[1:2, :]).astype(BF16)


def settle(own, place, pieces, weights, tokens, gains, others=()):
    rows, width = tokens.shape
    depth = weights[0].shape[1]
    tile = min(256, rows)
    steps = rows // tile
    wide = pl.BlockSpec((tile, width), lambda i: (i, 0))
    piece = pl.BlockSpec((tile, depth), lambda i: (i, 0))
    weight = pl.BlockSpec((width, depth), lambda i: (0, 0), pipeline_mode=pl.Buffered(1))
    return pl.pallas_call(
        functools.partial(settle_kernel, count=len(weights)),
        grid=(steps,),
        in_specs=[pl.BlockSpec((tile, depth), lambda i: (place * steps + i, 0))]
        + [piece] * len(pieces)
        + [weight] * len(weights)
        + [wide, pl.BlockSpec((8, width), lambda i: (0, 0))]
        + [ANYWHERE] * len(others),
        out_specs=[wide, wide],
        out_shape=[
            jax.ShapeDtypeStruct((rows, width), F32),
            jax.ShapeDtypeStruct((rows, width), BF16),
        ],
        compiler_params=limit(52),
        cost_estimate=declared(2 * len(weights) * rows * width * depth),
    )(own, *pieces, *weights, tokens, gains, *others)


def norm_back(grad_in, stream, gain):
    normed, scale_r = normalize(stream)
    scaled = grad_in * gain
    return scale_r * (scaled - normed * jnp.mean(scaled * normed, axis=-1, keepdims=True))


def settle_back_kernel(*refs, parts, count):
    terms, weights = refs[:parts], refs[parts : parts + count]
    grad_ref, stream_ref, gains_ref, out_ref, low_ref = refs[parts + count : parts + count + 5]
    pieces = refs[parts + count + 5 :]
    grad_in = terms[0][...].astype(F32)
    for term in terms[1:]:
        grad_in = grad_in + term[...].astype(F32)
    grad = grad_ref[...].astype(F32) + norm_back(grad_in, stream_ref[...], gains_ref[1:2, :])
    out_ref[...] = grad
    low = grad.astype(BF16)
    low_ref[...] = low
    for piece, weight in zip(pieces, weights):
        piece[...] = dot(low, weight[...]).astype(BF16)


def settle_back(terms, weights, grad, stream, gains):
    rows, width = grad.shape
    depth = weights[0].shape[1]
    tile = min(256, rows)
    wide = pl.BlockSpec((tile, width), lambda i: (i, 0))
    weight = pl.BlockSpec((width, depth), lambda i: (0, 0), pipeline_mode=pl.Buffered(1))
    return pl.pallas_call(
        functools.partial(settle_back_kernel, parts=len(terms), count=len(weights)),
        grid=(rows // tile,),
        in_specs=[wide] * len(terms)
        + [weight] * len(weights)
        + [wide, wide, pl.BlockSpec((8, width), lambda i: (0, 0))],
        out_specs=[wide, wide] + [pl.BlockSpec((tile, depth), lambda i: (i, 0))] * len(weights),
        out_shape=[
            jax.ShapeDtypeStruct((rows, width), F32),
            jax.ShapeDtypeStruct((rows, width), BF16),
        ]
        + [jax.ShapeDtypeStruct((rows, depth), BF16)] * len(weights),
        compiler_params=limit(52),
        cost_estimate=declared(2 * len(weights) * rows * width * depth),
    )(*terms, *weights, grad, stream, gains)


def causal(keys, queries):
    key = lax.broadcasted_iota(jnp.int32, (keys, queries), 0)
    return key <= lax.broadcasted_iota(jnp.int32, (keys, queries), 1)


def first_block(bound, offset, block):
    return jnp.where(offset >= bound, lax.div(bound, jnp.int32(block)), 0)


def attend_kernel(order_ref, q_ref, kx_ref, vt_ref, *rest, block):
    out_ref, lse_ref, top_ref, acc_ref = rest[-4:]
    kv = kx_ref.shape[0]
    per = q_ref.shape[1] // LANES // kv
    bound = order_ref[0]
    ones = jnp.ones((16, block), BF16)
    for group in range(kv):

        def q_step(turn, _):
            index = order_ref[1 + turn]
            offset = pl.multiple_of(index * block, block)
            into = pl.ds(pl.multiple_of(turn * block, block), block)
            top_ref[...] = jnp.full(top_ref.shape, MASKED, F32)
            acc_ref[...] = jnp.zeros(acc_ref.shape, F32)

            def tile(step, diagonal):
                keys = pl.ds(pl.multiple_of(step, block), block)
                value_t = jnp.concatenate(
                    [vt_ref[group * HD : (group + 1) * HD, keys], ones], axis=0
                )
                for head in range(2 * per):
                    column = (group * per + head // 2) * LANES
                    query = q_ref[pl.ds(offset, block), column : column + LANES]
                    scores = dot_cols(kx_ref[group, head % 2, keys, :], query)
                    if diagonal:
                        scores = jnp.where(causal(block, block), scores, MASKED)
                    old = top_ref[head, 0:1, :]
                    top = jnp.maximum(old, jnp.max(scores, axis=0, keepdims=True))
                    powered = jnp.exp(scores - top).astype(BF16)
                    acc_ref[head] = acc_ref[head] * jnp.exp(old - top) + dot(value_t, powered)
                    top_ref[head, 0:1, :] = top

            def full_tile(step, carry):
                tile(step * block, False)
                return carry

            lax.fori_loop(first_block(bound, offset, block), index, full_tile, 0)
            tile(offset, True)
            for pair in range(per):
                both = []
                for head in (2 * pair, 2 * pair + 1):
                    total = acc_ref[head, HD : HD + 1, :]
                    both.append(acc_ref[head, :HD, :] / total)
                    place = group * 2 * per + head
                    lse_ref[place : place + 1, into] = top_ref[
                        head, 0:1, :
                    ] + jnp.log(total)
                column = (group * per + pair) * LANES
                out_ref[into, column : column + LANES] = (
                    jnp.concatenate(both, axis=0).T.astype(BF16)
                )
            return _

        lax.fori_loop(0, out_ref.shape[0] // block, q_step, 0)


def attend(bound, order, queries, kx, vt, block, others=()):
    length, width = queries.shape
    heads = width // HD
    kv = kx.shape[0]
    per = heads // kv
    count = len(order)
    cells = heads * count * block * (length + block) // 2
    vmem = pl.BlockSpec(memory_space=pltpu.VMEM)
    return pl.pallas_call(
        functools.partial(attend_kernel, block=block),
        in_specs=[pl.BlockSpec(memory_space=pltpu.SMEM), vmem, vmem, vmem] + [ANYWHERE] * len(others),
        out_specs=[vmem, vmem],
        out_shape=[
            jax.ShapeDtypeStruct((count * block, width), BF16),
            jax.ShapeDtypeStruct((heads, count * block), F32),
        ],
        scratch_shapes=[
            pltpu.VMEM((per, 8, block), F32),
            pltpu.VMEM((per, HD + 16, block), F32),
        ],
        compiler_params=limit(52),
        cost_estimate=declared(2 * 4 * HD * 4 * cells, 16),
    )(jnp.stack([bound, *order]), queries, kx, vt, *others)


def attend_back_kernel(
    order_ref, q_ref, kx_ref, vx_ref, kt_ref, lse_ref, out_ref, grad_ref, cos_ref, sin_ref,
    *rest, block
):
    dqkv_ref, dk_ref, dv_ref, dq_ref = rest[-4:]
    length = q_ref.shape[0]
    kv = kx_ref.shape[0]
    heads = q_ref.shape[1] // HD
    per = heads // 2 // kv
    bound = order_ref[0]
    dk_ref[...] = jnp.zeros(dk_ref.shape, F32)
    dv_ref[...] = jnp.zeros(dv_ref.shape, F32)
    lane = lax.broadcasted_iota(jnp.int32, (8, LANES), 1)
    row = lax.broadcasted_iota(jnp.int32, (8, LANES), 0)
    chosen = ((lane // HD) == row).astype(F32)

    def turn_back(values, rows):
        return values * cos_ref[rows, :] - swap_halves(values) * sin_ref[rows, :]

    for group in range(kv):

        def q_step(turn, _):
            index = order_ref[1 + turn]
            offset = pl.multiple_of(index * block, block)
            rows = pl.ds(offset, block)
            given = pl.ds(pl.multiple_of(turn * block, block), block)
            dq_ref[...] = jnp.zeros(dq_ref.shape, F32)
            deltas = []
            for pair in range(per):
                column = (group * per + pair) * LANES
                product = grad_ref[given, column : column + LANES].astype(F32) * out_ref[
                    given, column : column + LANES
                ].astype(F32)
                deltas.append(
                    lax.dot_general(
                        chosen, product, OVER_COLS, precision=lax.Precision.HIGHEST,
                        preferred_element_type=F32,
                    )
                )

            def tile(step, size, skip, diagonal):
                keys = pl.ds(pl.multiple_of(step, size), size)
                key_t = kt_ref[group * HD : (group + 1) * HD, keys]
                mine = pl.ds(offset + skip, block - skip)
                theirs = pl.ds(turn * block + skip, block - skip)
                for parity in range(2):
                    key_add, value_add = 0.0, 0.0
                    for pair in range(per):
                        head = 2 * pair + parity
                        place = group * 2 * per + head
                        column = (group * per + pair) * LANES
                        query = q_ref[mine, column : column + LANES]
                        grad = grad_ref[theirs, column : column + LANES]
                        scores = dot_cols(kx_ref[group, parity, keys, :], query)
                        if diagonal:
                            scores = jnp.where(causal(size, block - skip), scores, MASKED)
                        probs = jnp.exp(scores - lse_ref[place : place + 1, given][:, skip:])
                        dprobs = dot_cols(vx_ref[group, parity, keys, :], grad)
                        delta = deltas[pair][parity : parity + 1, skip:]
                        dscores = (probs * (dprobs - delta)).astype(BF16)
                        value_add = value_add + dot(probs.astype(BF16), grad)
                        key_add = key_add + dot(dscores, query)
                        dq_ref[head * HD : (head + 1) * HD, skip:] += dot(key_t, dscores)
                    dk_ref[group, parity, keys, :] += key_add
                    dv_ref[group, parity, keys, :] += value_add

            def full_tile(step, carry):
                tile(step * block, block, 0, False)
                return carry

            lax.fori_loop(first_block(bound, offset, block), index, full_tile, 0)
            tile(offset, block // 2, 0, True)
            tile(offset + block // 2, block // 2, block // 2, True)
            for pair in range(per):
                column = (group * per + pair) * LANES
                grad_q = dq_ref[pair * LANES : (pair + 1) * LANES, :].T * (1.0 / math.sqrt(HD))
                dqkv_ref[rows, column : column + LANES] = turn_back(grad_q, rows).astype(BF16)
            return _

        lax.fori_loop(0, length // block, q_step, 0)

    def finish(index, _):
        rows = pl.ds(pl.multiple_of(index * block, block), block)
        lanes = lax.broadcasted_iota(jnp.int32, (block, LANES), 1)

        def placed(part, half):
            ref = dk_ref if part < kv else dv_ref
            even, odd = ref[part % kv, 0, rows, :], ref[part % kv, 1, rows, :]
            return even + pltpu.roll(odd, HD, 1) if half == 0 else pltpu.roll(even, HD, 1) + odd

        for chunk in range(kv):
            values = jnp.where(lanes < HD, placed(2 * chunk, 0), placed(2 * chunk + 1, 1))
            if 2 * chunk + 1 < kv:
                values = turn_back(values, rows)
            elif 2 * chunk < kv:
                values = jnp.where(lanes < HD, turn_back(values, rows), values)
            column = heads * HD + chunk * LANES
            dqkv_ref[rows, column : column + LANES] = values.astype(BF16)
        return _

    lax.fori_loop(0, length // block, finish, 0)


def attend_back(
    bound, order, queries, kx, vx, kt, log_sums, attended, grad, cosine, sine, block, others
):
    length, width = queries.shape
    heads = width // HD
    kv = kx.shape[0]
    cells = heads * length * (length + block) // 2
    vmem = pl.BlockSpec(memory_space=pltpu.VMEM)
    return pl.pallas_call(
        functools.partial(attend_back_kernel, block=block),
        in_specs=[pl.BlockSpec(memory_space=pltpu.SMEM)] + [vmem] * 9 + [ANYWHERE] * len(others),
        out_specs=vmem,
        out_shape=jax.ShapeDtypeStruct((length, width + 2 * kv * HD), BF16),
        scratch_shapes=[
            pltpu.VMEM((kv, 2, length, LANES), F32),
            pltpu.VMEM((kv, 2, length, LANES), F32),
            pltpu.VMEM((heads // kv * HD, block), F32),
        ],
        compiler_params=limit(52),
        cost_estimate=declared(2 * 10 * HD * 4 * cells),
    )(jnp.stack([bound, *order]), queries, kx, vx, kt, log_sums, attended, grad, cosine, sine, *others)


def local(
    inputs,
    segment_ids,
    attn_gain,
    query_weight,
    key_weight,
    value_weight,
    output_weight,
    mlp_gain,
    gate_weight,
    up_weight,
    down_weight,
    cotangent,
    *,
    sizes,
):
    rows = inputs.shape[0]
    length = segment_ids.shape[0]
    query_cols = query_weight.shape[1]
    key_cols = key_weight.shape[1]
    heads, kv = query_cols // HD, key_cols // HD
    columns = query_cols + 2 * key_cols
    slots = slots_of(sizes["tensor"])
    tensor = sizes["tensor"]
    space = (-columns) % query_cols or query_cols
    gains = jnp.pad(jnp.stack([attn_gain, mlp_gain], axis=1), ((0, 0), (0, space - 2)))
    bundle = lax.all_gather(
        jnp.concatenate([query_weight, key_weight, value_weight, gains, output_weight.T], axis=1),
        "dp", axis=0, tiled=True,
    )
    out_own = bundle[:, columns + space :]
    hop = first_hop(inputs, tensor)
    gate_up = lax.all_gather(
        hold(jnp.concatenate([gate_weight, up_weight], axis=1), *(hop or ())),
        "dp", axis=0, tiled=True,
    )

    bound, cosine, sine = rope_tables(segment_ids)
    blocks = second_hop(inputs, hop, tensor)
    stream = inputs.astype(F32)
    arrays = project(slots, blocks, bundle, cosine, sine, heads, kv, length)
    block_a, queries, kx, vx, kt, vt, gains = arrays
    down_t = lax.all_gather(turn(down_weight, [queries]), "dp", axis=0, tiled=True)

    if tensor == 4:
        out_own = hold(out_own, blocks[3])
        out_hop = first_hop(out_own, tensor)
        far, far_sums = attend(bound, slots[3:], queries, kx, vt, rows)
        from_far = lax.ppermute(far, "tensor", pairs(tensor, 3))
        first, first_sums = attend(bound, slots[1:2], queries, kx, vt, rows, [far])
        from_one = lax.ppermute(first, "tensor", pairs(tensor, 1))
        halves = hold_halves(out_hop, first)
        out_all = second_hop(out_own, out_hop, tensor, halves)
        second, second_sums = attend(bound, slots[2:3], queries, kx, vt, rows, halves)
        from_two = lax.ppermute(second, "tensor", pairs(tensor, 2))
        own, own_sums = attend(bound, slots[:1], queries, kx, vt, rows, [second])
        stream_one, low_m = settle(own, 0, [from_one, from_two, from_far], out_all, inputs, gains)
        order = [slots[1], slots[2], slots[0], slots[3]]
        attended = jnp.concatenate([first, second, own, far], axis=0)
        log_sums = jnp.concatenate([first_sums, second_sums, own_sums, far_sums], axis=1)
    else:
        order = slots
        out_all = gather(out_own, tensor)
        attended, log_sums = attend(bound, order, queries, kx, vt, rows)
        given = trade([attended[k * rows : (k + 1) * rows] for k in range(tensor)], tensor)
        stream_one, low_m = settle(given[0], 0, given[1:], out_all, inputs, gains)
        cotangent_sent = cotangent
    parts_m = [low_m]
    units = gate_weight.shape[1]

    def feed_at(place, wanted, fed, others=()):
        return feed(
            feed_kernel, place, tensor, [parts_m[k] for k in wanted], [gate_up] * 2, [0, 1], [],
            units, 3, True, 512, fed, others,
        )

    def back_m(places, fed, into=None, others=(), split=False):
        return back(places, rows, fed[:2], [gate_up] * 2, [0, 1], into, others, split)

    def back_out(places, into=None, others=(), split=False):
        return back(places, rows, [hidden], [down_t], [0], into, others, split)

    def reduce_rows(term, *others):
        if others and tensor == 4:
            term = hold(term, *others)
        return lax.psum_scatter(term, "dp", scatter_dimension=0, tiled=True)

    if tensor == 4:
        hop = first_hop(parts_m[0], tensor)
        cotangent_sent = hold(cotangent, *hop)
        cotangent_hop = first_hop(cotangent_sent, tensor)
        fed = feed_at(3, [0], None)
        parts_m = second_hop(parts_m[0], hop, tensor)
        fed = feed_at(0, [1, 2], fed)
        halves = hold_halves(cotangent_hop, fed[0])
        grad_parts = second_hop(cotangent_sent, cotangent_hop, tensor, halves)
        fed = feed_at(2, [3], fed, halves)
    else:
        grad_parts = second_hop(cotangent_sent, None, tensor)
        parts_m = gather(parts_m[0], tensor)
        fed = None
        for place in range(tensor):
            fed = feed_at(place, [place], fed)
    hidden, silu, slope, block_m = fed
    places = [1, 2, 3, 0] if tensor == 4 else list(range(tensor))
    grad_parts = [grad_parts[k] for k in places]

    def feed_back(others=()):
        return feed(
            feed_back_kernel, 0, tensor, grad_parts, [down_t], [0], [silu, slope], units, 2, False, 512,
            None, others,
        )

    if tensor == 4:
        three_out = back_out([2], None, [fed[0]], True)
        out_one, out_two = out_halves = send_half(three_out, tensor)
        down_t_wgrad = weigh(grad_parts, hidden, three_out[:1])
        one_out, two_out, own_out = back_out(
            [0, 1, 3], [(out_one, False), (out_two, True), None]
        )
        out_parts = [
            own_out,
            lax.ppermute(one_out, "tensor", pairs(tensor, 1)),
            lax.ppermute(two_out, "tensor", pairs(tensor, 2)),
        ]
        fed = feed_back([one_out])
        three_m = back_m([2], fed, None, (), True)
        m_one, m_two = m_halves = send_half(three_m, tensor)
        gate_wgrad = weigh([block_m], fed[0], [three_m[0], *out_parts[1:]])
        one_m, two_m = back_m([0, 1], fed, [(m_one, False), (m_two, True)])
        (own_m,) = back_m([3], fed, None, [one_m])
        up_wgrad = weigh([block_m], fed[1], [own_m])
        grad_m_parts = [
            own_m,
            lax.ppermute(one_m, "tensor", pairs(tensor, 1)),
            lax.ppermute(two_m, "tensor", pairs(tensor, 2)),
        ]
    else:
        down_t_wgrad = weigh(grad_parts, hidden)
        fed = feed_back()
        grad_m_parts = sum_whole(back_m(list(range(tensor)), fed))
        gate_wgrad, up_wgrad = weigh([block_m], fed[0]), weigh([block_m], fed[1])
        out_parts = sum_whole(back_out(list(range(tensor))))
    layer_out = (stream_one + total(out_parts)).astype(BF16)
    if tensor != 4:
        out_halves = m_halves = ()
    down_t_low = reduce_rows(down_t_wgrad, *out_halves)
    gate_low = reduce_rows(gate_wgrad, *m_halves)
    up_low = reduce_rows(up_wgrad, *grad_m_parts[1:])

    grad_stream_one, grad_stream_low, *pieces = settle_back(
        grad_m_parts, out_all, cotangent, stream_one, gains
    )
    given = trade(pieces, tensor)
    places = [1, 2, 0, 3] if tensor == 4 else list(range(tensor))
    grad_attended = jnp.concatenate([given[k] for k in places], axis=0)
    grad_qkv = attend_back(
        bound, order, queries, kx, vx, kt, log_sums, attended, grad_attended, cosine, sine, rows,
        [down_t_low],
    )
    if tensor == 4:
        sent = hold(grad_stream_low, grad_attended)
        grad_stream_parts = trade([sent] * 4, tensor)
    else:
        grad_stream_parts = gather(grad_stream_low, tensor)
    grad_stream_parts = [grad_stream_parts[k] for k in places]

    def back_a(places, others=(), split=False):
        return back(places, rows, [grad_qkv], [bundle], [0], None, others, split)

    if tensor == 4:
        three = back_a(slots[3:], [gate_low], True)
        halves = send_half(three, tensor)
        block_a = hold(block_a, three[0])
    attention_wgrad = weigh_both(block_a, grad_qkv, grad_stream_parts, attended)
    gate_sum, up_sum, down_t_sum = [low.astype(F32) for low in (gate_low, up_low, down_t_low)]
    if tensor == 4:
        attention_wgrad = hold(attention_wgrad, *halves)
    attention_sum = reduce_rows(attention_wgrad).astype(F32)
    if tensor == 4:
        one, two, own = back_a([slots[1], slots[2], slots[0]], three[:1])
        grad_a_parts = [own, *send_whole(one, two, halves, tensor)]
    else:
        grad_a_parts = sum_whole(back_a(slots))
    grad_normed_a = total(grad_a_parts)

    product = attention_wgrad[:, :columns].astype(F32) * bundle[:, :columns].astype(F32)
    attn_term = sum_tensor(jnp.sum(product, axis=1)[None, :], tensor)
    width = attn_gain.shape[0]
    attn_term = lax.dynamic_slice_in_dim(
        sum_blocks(attn_term, sizes["dp"]), lax.axis_index("dp") * width, width, 1
    )

    def gain_term(gain, weights):
        term = sum(jnp.sum(weight.astype(F32) * grad, axis=1) for weight, grad in weights)
        return term / gain.astype(F32)

    query_sum = attention_sum[:, :query_cols]
    key_sum = attention_sum[:, query_cols : query_cols + key_cols]
    value_sum = attention_sum[:, query_cols + key_cols : columns]
    mlp_term = sum_tensor(
        gain_term(mlp_gain, [(gate_weight, gate_sum), (up_weight, up_sum)])[None, :], tensor
    )
    input_grad = (grad_stream_one + norm_back(grad_normed_a, stream, gains[0:1])).astype(BF16)
    return (
        layer_out,
        input_grad,
        attn_term[0] / attn_gain.astype(F32),
        query_sum,
        key_sum,
        value_sum,
        attention_sum[:, columns:].T,
        mlp_term[0],
        gate_sum,
        up_sum,
        down_t_sum.T,
    )


def solution(mesh):
    tokens = P(("dp", "tensor"), None)
    in_specs = (
        tokens,
        P("dp"),
        P("dp"),
        P("dp", "tensor"),
        P("dp", "tensor"),
        P("dp", "tensor"),
        P("tensor", "dp"),
        P("dp"),
        P("dp", "tensor"),
        P("dp", "tensor"),
        P("tensor", "dp"),
        tokens,
    )
    out_specs = (
        tokens,
        tokens,
        P("dp"),
        P("dp", "tensor"),
        P("dp", "tensor"),
        P("dp", "tensor"),
        P("tensor", "dp"),
        P("dp"),
        P("dp", "tensor"),
        P("dp", "tensor"),
        P("tensor", "dp"),
    )
    return jax.shard_map(
        functools.partial(local, sizes={axis: mesh.shape[axis] for axis in ("tensor", "dp")}),
        mesh=mesh, in_specs=in_specs, out_specs=out_specs, check_vma=False,
    )
```

profile of v0, /device:TPU:26, one launch (start us, length us, event | category | flops | bytes accessed | tf_op | source)
XLA Modules:
  0.0 801.3 jit_solution(3702469990691204583)
XLA Ops:
  21.0 40.3 %collective-permute-done.value_ref.refs_1_ = bf16[512,2048]{1,0:T(8,128)(2,1)} collective-permute-done((bf16[512,2048]{1,0:T(8,128)(2,1)S(1)}, bf16[512,2048]{1,0:T(8,128)(2,1)}, u32[]{:S(2)}, u32[]{:S(2)}) %collective-permute-start) | collective-permute-done | bytes 2097184 | tf_op jit(solution)/shard_map/ppermute | solution.py:78
  73.1 13.6 %collective-permute-done.2 = bf16[256,2048]{1,0:T(8,128)(2,1)} collective-permute-done((bf16[256,2048]{1,0:T(8,128)(2,1)S(1)}, bf16[256,2048]{1,0:T(8,128)(2,1)}, u32[]{:S(2)}, u32[]{:S(2)}) %collective-permute-start.2) | collective-permute-done | bytes 1048608 | tf_op jit(solution)/shard_map/ppermute | solution.py:110
  96.1 19.0 %shard_map.205 = (bf16[2048,2048]{1,0:T(8,128)(2,1)}, bf16[2048,512]{1,0:T(8,128)(2,1)}, bf16[2,2,2048,128]{3,2,1,0:T(8,128)(2,1)}, bf16[2,2,2048,128]{3,2,1,0:T...) custom-call(s32[4]{0:T(128)S(1)} %pad_add_fusion.1.slot_ref, ...), custom_call_target="tpu_custom_call" | custom-call | flops 402653184 | tf_op jit(solution)/shard_map/pallas_call | solution.py:287
  116.0 15.5 %shard_map.207 = (bf16[512,512]{1,0:T(8,128)(2,1)}, f32[8,512]{1,0:T(8,128)S(1)}) custom-call(s32[2]{0:T(128)S(1)} %pad_add_fusion.4.order_ref, bf16[2048,512]{1,0:T(8,128)(2,1)} %get-tuple-element.62.q_ref.rest_0_, bf16[2,2,2048,128]{3,2,1,0:T(8,128)(2,1)} %get-tuple-element.63.kx_ref, bf16[128,2048]{1,0:T(8,128)(2,1)S(1)} %get-tuple-element.64.vt_ref), custom_call_target="tpu_custom_call" | custom-call | flops 171798691840 | tf_op jit(solution)/shard_map/pallas_call | solution.py:695
  164.2 19.9 %shard_map.211 = (bf16[512,512]{1,0:T(8,128)(2,1)}, f32[8,512]{1,0:T(8,128)S(1)}) custom-call(s32[2]{0:T(128)S(1)} %pad_add_fusion.2.order_ref, bf16[2048,512]{1,0:T(8,128)(2,1)} %get-tuple-element.62.q_ref.rest_0_, bf16[2,2,2048,128]{3,2,1,0:T(8,128)(2,1)} %get-tuple-element.63.kx_ref, bf16[128,2048]{1,0:T(8,128)(2,1)S(1)} %get-tuple-element.64.vt_ref, ...), custom_call_target="tpu_custom_call" | custom-call | flops 171798691840 | tf_op jit(solution)/shard_map/pallas_call | solution.py:695
  184.1 10.5 %shard_map.212 = (bf16[512,512]{1,0:T(8,128)(2,1)S(1)}, f32[8,512]{1,0:T(8,128)S(1)}) custom-call(s32[2]{0:T(128)S(1)} %get-tuple-element.154.order_ref, bf16[2048,512]{1,0:T(8,128)(2,1)} %get-tuple-element.62.q_ref.rest_0_, bf16[2,2,2048,128]{3,2,1,0:T(8,128)(2,1)} %get-tuple-element.63.kx_ref, bf16[128,2048]{1,0:T(8,128)(2,1)S(1)} %get-tuple-element.64.vt_ref, ...), custom_call_target="tpu_custom_call" | custom-call | flops 171798691840 | tf_op jit(solution)/shard_map/pallas_call | solution.py:695
  198.7 11.3 %shard_map.213 = (f32[512,2048]{1,0:T(8,128)}, bf16[512,2048]{1,0:T(8,128)(2,1)}) custom-call(bf16[512,512]{1,0:T(8,128)(2,1)S(1)} %get-tuple-element.68.refs_0_, bf16[512,512]{1,0:T(8,128)(2,1)} %collective-permute-done.6.refs_1_, bf16[512,512]{1,0:T(8,128)(2,1)} %collective-permute-done.7.refs_2_, bf16[512,512]{1,0:T(8,128)(2,1)} %collective-permute-done.8.refs_3_, ...), custom_call_target="tpu_custom_call" | custom-call | flops 268435456 | tf_op jit(solution)/shard_map/pallas_call | solution.py:560
  221.8 40.9 %collective-permute-done.13.value_ref.refs_1_.refs_2_ = bf16[512,2048]{1,0:T(8,128)(2,1)S(1)} collective-permute-done((bf16[512,2048]{1,0:T(8,128)(2,1)}, bf16[512,2048]{1,0:T(8,128)(2,1)S(1)}, u32[]{:S(2)}, u32[]{:S(2)}) %collective-permute-start.13) | collective-permute-done | bytes 2097184 | tf_op jit(solution)/shard_map/ppermute | solution.py:78
  273.2 15.8 %shard_map.217 = (bf16[2048,2048]{1,0:T(8,128)(2,1)}, bf16[2048,2048]{1,0:T(8,128)(2,1)}, bf16[2048,2048]{1,0:T(8,128)(2,1)}, bf16[2048,2048]{1,0:T(8,128)(2,1)}) custom-call(bf16[512,2048]{1,0:T(8,128)(2,1)} %get-tuple-element.71.refs_0_, bf16[2048,4096]{1,0:T(8,128)(2,1)} %all-gather.6.cloned.1.call-done.refs_1_.refs_2_.refs_3_.refs_4_.refs_5_, ...), custom_call_target="tpu_custom_call" | custom-call | flops 536870912 | tf_op jit(solution)/shard_map/pallas_call | solution.py:363
  289.1 25.7 %shard_map.218 = (bf16[2048,2048]{1,0:T(8,128)(2,1)}, bf16[2048,2048]{1,0:T(8,128)(2,1)}, bf16[2048,2048]{1,0:T(8,128)(2,1)}, bf16[2048,2048]{1,0:T(8,128)(2,1)}) custom-call(bf16[512,2048]{1,0:T(8,128)(2,1)} %collective-permute-done.11.value_ref.refs_0_.refs_1_, ...), custom_call_target="tpu_custom_call", output_to_operand_aliasing={{0}: (4, {}), {1}: (5, {}), {2}: (6, {}), {3}: (7, {})} | custom-call | flops 1073741824 | tf_op jit(solution)/shard_map/pallas_call | solution.py:363
  318.0 19.1 %collective-permute-done.14 = bf16[256,2048]{1,0:T(8,128)(2,1)} collective-permute-done((bf16[256,2048]{1,0:T(8,128)(2,1)S(1)}, bf16[256,2048]{1,0:T(8,128)(2,1)}, u32[]{:S(2)}, u32[]{:S(2)}) %collective-permute-start.14) | collective-permute-done | bytes 1048608 | tf_op jit(solution)/shard_map/ppermute | solution.py:111
  340.5 15.6 %shard_map.222 = (bf16[2048,2048]{1,0:T(8,128)(2,1)}, bf16[2048,2048]{1,0:T(8,128)(2,1)}, bf16[2048,2048]{1,0:T(8,128)(2,1)}, bf16[2048,2048]{1,0:T(8,128)(2,1)}) custom-call(bf16[512,2048]{1,0:T(8,128)(2,1)} %pad_maximum_fusion.refs_0_, ...), custom_call_target="tpu_custom_call", output_to_operand_aliasing={{0}: (3, {}), {1}: (4, {}), {2}: (5, {}), {3}: (6, {})} | custom-call | flops 536870912 | tf_op jit(solution)/shard_map/pallas_call | solution.py:363
  370.9 25.7 %shard_map.231.refs_0_ = bf16[2048,2048]{1,0:T(8,128)(2,1)} custom-call(bf16[512,2048]{1,0:T(8,128)(2,1)} %collective-permute-done.15.value_ref.refs_0_, bf16[512,2048]{1,0:T(8,128)(2,1)} %collective-permute-done.16.value_ref.refs_1_, bf16[512,2048]{1,0:T(8,128)(2,1)} %copy-done.19, bf16[512,2048]{1,0:T(8,128)(2,1)} %shard_map.219.refs_3_, ...), custom_call_target="tpu_custom_call" | custom-call | flops 1073741824 | tf_op jit(solution)/shard_map/pallas_call | solution.py:495
  398.8 19.1 %shard_map.225 = (bf16[512,2048]{1,0:T(8,128)(2,1)}, bf16[512,2048]{1,0:T(8,128)(2,1)}, bf16[512,2048]{1,0:T(8,128)(2,1)}) custom-call(s32[3]{0:T(128)S(1)} %copy-done.12, bf16[2048,2048]{1,0:T(8,128)(2,1)} %get-tuple-element.80.refs_0_.refs_2_.refs_1_.refs_4_, bf16[2048,2048]{1,0:T(8,128)(2,1)} %get-tuple-element.80.refs_0_.refs_2_.refs_1_.refs_4_, ...), custom_call_target="tpu_custom_call" | custom-call | flops 805306368 | tf_op jit(solution)/shard_map/pallas_call | solution.py:420
  420.0 27.1 %shard_map.226 = (bf16[2048,2048]{1,0:T(8,128)(2,1)}, bf16[2048,2048]{1,0:T(8,128)(2,1)}) custom-call(bf16[512,2048]{1,0:T(8,128)(2,1)} %collective-permute-done.15.value_ref.refs_0_, bf16[512,2048]{1,0:T(8,128)(2,1)} %collective-permute-done.16.value_ref.refs_1_, bf16[512,2048]{1,0:T(8,128)(2,1)} %copy-done.19, bf16[512,2048]{1,0:T(8,128)(2,1)} %shard_map.219.refs_3_, ...), custom_call_target="tpu_custom_call" | custom-call | flops 1073741824 | tf_op jit(solution)/shard_map/pallas_call | solution.py:363
  447.1 13.9 %shard_map.227 = (bf16[256,2048]{1,0:T(8,128)(2,1)S(1)}, bf16[256,2048]{1,0:T(8,128)(2,1)}) custom-call(s32[1]{0:T(128)} %constant.60.clone.1.slot_ref, bf16[2048,2048]{1,0:T(8,128)(2,1)} %get-tuple-element.88.refs_0_.refs_2_.refs_1_, bf16[2048,2048]{1,0:T(8,128)(2,1)} %get-tuple-element.89.refs_1_.refs_3_, ...), custom_call_target="tpu_custom_call" | custom-call | flops 536870912 | tf_op jit(solution)/shard_map/pallas_call | solution.py:420
  465.1 25.8 %shard_map.234.refs_0_ = bf16[2048,2048]{1,0:T(8,128)(2,1)} custom-call(bf16[2048,2048]{1,0:T(8,128)(2,1)} %get-tuple-element.105.refs_0_, bf16[2048,2048]{1,0:T(8,128)(2,1)} %get-tuple-element.88.refs_0_.refs_2_.refs_1_, bf16[256,2048]{1,0:T(8,128)(2,1)S(1)} %get-tuple-element.91.refs_2_, bf16[512,2048]{1,0:T(8,128)(2,1)} %copy-done.26, ...), custom_call_target="tpu_custom_call" | custom-call | flops 1073741824 | tf_op jit(solution)/shard_map/pallas_call | solution.py:495
  494.1 24.9 %shard_map.228 = (bf16[512,2048]{1,0:T(8,128)(2,1)}, bf16[512,2048]{1,0:T(8,128)(2,1)}) custom-call(s32[2]{0:T(128)S(1)} %iota.41.slot_ref, bf16[2048,2048]{1,0:T(8,128)(2,1)} %get-tuple-element.88.refs_0_.refs_2_.refs_1_, bf16[2048,2048]{1,0:T(8,128)(2,1)} %get-tuple-element.89.refs_1_.refs_3_, ...), custom_call_target="tpu_custom_call" | custom-call | flops 1073741824 | tf_op jit(solution)/shard_map/pallas_call | solution.py:420
  521.0 13.9 %shard_map.229.refs_0_.refs_2_ = bf16[512,2048]{1,0:T(8,128)(2,1)} custom-call(s32[1]{0:T(128)} %constant.61.clone.1.slot_ref, bf16[2048,2048]{1,0:T(8,128)(2,1)} %get-tuple-element.88.refs_0_.refs_2_.refs_1_, bf16[2048,2048]{1,0:T(8,128)(2,1)} %get-tuple-element.89.refs_1_.refs_3_, ...), custom_call_target="tpu_custom_call" | custom-call | flops 536870912 | tf_op jit(solution)/shard_map/pallas_call | solution.py:420
  534.9 25.4 %shard_map.242.refs_0_ = bf16[2048,2048]{1,0:T(8,128)(2,1)} custom-call(bf16[2048,2048]{1,0:T(8,128)(2,1)} %get-tuple-element.105.refs_0_, bf16[2048,2048]{1,0:T(8,128)(2,1)} %get-tuple-element.89.refs_1_.refs_3_, bf16[512,2048]{1,0:T(8,128)(2,1)} %shard_map.229.refs_0_.refs_2_), custom_call_target="tpu_custom_call" | custom-call | flops 1073741824 | tf_op jit(solution)/shard_map/pallas_call | solution.py:495
  562.5 13.7 %shard_map.230 = (f32[512,2048]{1,0:T(8,128)}, bf16[512,2048]{1,0:T(8,128)(2,1)}, bf16[512,512]{1,0:T(8,128)(2,1)S(1)}, bf16[512,512]{1,0:T(8,128)(2,1)S(1)}, bf...) custom-call(bf16[512,2048]{1,0:T(8,128)(2,1)} %shard_map.229.refs_0_.refs_2_, bf16[512,2048]{1,0:T(8,128)(2,1)} %copy-done.21, ...), custom_call_target="tpu_custom_call" | custom-call | flops 268435456 | tf_op jit(solution)/shard_map/pallas_call | solution.py:605
  610.0 72.2 %shard_map.233.refs_0_.refs_1_.refs_2_.refs_5_ = bf16[2048,768]{1,0:T(8,128)(2,1)} custom-call(s32[5]{0:T(128)S(1)} %stack.75.order_ref, bf16[2048,512]{1,0:T(8,128)(2,1)} %get-tuple-element.62.q_ref.rest_0_, bf16[2,2,2048,128]{3,2,1,0:T(8,128)(2,1)} %get-tuple-element.63.kx_ref, bf16[2,2,2048,128]{3,2,1,0:T(8,128)(2,1)} %get-tuple-element.95.vx_ref, ...), custom_call_target="tpu_custom_call" | custom-call | flops 6710886400 | tf_op jit(solution)/shard_map/pallas_call | solution.py:823
  692.5 17.0 %shard_map.240.refs_0_ = bf16[2048,1280]{1,0:T(8,128)(2,1)} custom-call(bf16[2048,2048]{1,0:T(8,128)(2,1)} %shard_map.238.refs_0_, bf16[512,2048]{1,0:T(8,128)(2,1)} %collective-permute-done.34.refs_1_, bf16[512,2048]{1,0:T(8,128)(2,1)} %collective-permute-done.35.refs_2_, bf16[512,2048]{1,0:T(8,128)(2,1)} %shard_map.239.refs_3_, ...), custom_call_target="tpu_custom_call" | custom-call | flops 671088640 | tf_op jit(solution)/shard_map/pallas_call | solution.py:526
  758.9 16.3 %collective-permute-done.45 = f32[1,256]{1,0:T(1,128)S(1)} collective-permute-done((f32[1,256]{1,0:T(1,128)S(1)}, f32[1,256]{1,0:T(1,128)S(1)}, u32[]{:S(2)}, u32[]{:S(2)}) %collective-permute-start.45) | collective-permute-done | bytes 1056 | tf_op jit(solution)/shard_map/ppermute | solution.py:160
  (299 shorter events, 243.6 us)
Async XLA Ops:
  7.2 83.6 %all-gather.4.cloned.1.call-start = ((), (), s32[]{:S(2)}) async-start(), calls=%async_computation.4 | async-start | bytes 7077888 | tf_op jit(solution)/shard_map/all_gather | solution.py:864
  13.6 259.6 %all-gather.6.cloned.1.call-start = ((), (), s32[]{:S(2)}) async-start(), calls=%async_computation.5 | async-start | bytes 18874368 | tf_op jit(solution)/shard_map/all_gather | solution.py:870
  13.7 47.5 %collective-permute-start = (bf16[512,2048]{1,0:T(8,128)(2,1)S(1)}, bf16[512,2048]{1,0:T(8,128)(2,1)}, u32[]{:S(2)}, u32[]{:S(2)}) collective-permute-start(bf16[512,2048]{1,0:T(8,128)(2,1)S(1)} %copy-done.15), channel_id=1, source_target_pairs={{0,1},{1,0},{2,3},{3,2},{4,5},{5,4},{6,7},{7,6},{8,9},{9,8},{10,11... | collective-permute-start | bytes 6291464 | tf_op jit(solution)/shard_map/ppermute | solution.py:78
  14.3 49.9 %collective-permute-start.1 = (bf16[512,2048]{1,0:T(8,128)(2,1)S(1)}, bf16[512,2048]{1,0:T(8,128)(2,1)}, u32[]{:S(2)}, u32[]{:S(2)}) collective-permute-start(bf16[512,2048]{1,0:T(8,128)(2,1)S(1)} %copy-done.15), channel_id=1, source_target_pairs={{0,2},{1,3},{2,0},{3,1},{4,6},{5,7},{6,4},{7,5},{8,10},{9,11},{10,... | collective-permute-start | bytes 6291464 | tf_op jit(solution)/shard_map/ppermute | solution.py:78
  73.1 283.1 %all-gather.8.cloned.1.call-start = ((), (), s32[]{:S(2)}) async-start(), calls=%async_computation.6 | async-start | bytes 9437184 | tf_op jit(solution)/shard_map/all_gather | solution.py:880
  95.0 57.4 %collective-permute-start.4 = (bf16[2048,512]{1,0:T(8,128)(2,1)}, bf16[2048,512]{1,0:T(8,128)(2,1)}, u32[]{:S(2)}, u32[]{:S(2)}) collective-permute-start(bf16[2048,512]{1,0:T(8,128)(2,1)} %shard_map.206.refs_4_.refs_3_), channel_id=1, source_target_pairs={{0,1},{1,0},{2,3},{3,2},{4,5},{5,4},{6,7},{7,6},{8,9},{9,8},{10,11... | collective-permute-start | bytes 6291464 | tf_op jit(solution)/shard_map/ppermute | solution.py:78
  95.6 64.9 %collective-permute-start.5 = (bf16[2048,512]{1,0:T(8,128)(2,1)}, bf16[2048,512]{1,0:T(8,128)(2,1)}, u32[]{:S(2)}, u32[]{:S(2)}) collective-permute-start(bf16[2048,512]{1,0:T(8,128)(2,1)} %shard_map.206.refs_4_.refs_3_), channel_id=1, source_target_pairs={{0,2},{1,3},{2,0},{3,1},{4,6},{5,7},{6,4},{7,5},{8,10},{9,11},{10,... | collective-permute-start | bytes 6291464 | tf_op jit(solution)/shard_map/ppermute | solution.py:78
  131.5 65.9 %collective-permute-start.8 = (bf16[512,512]{1,0:T(8,128)(2,1)}, bf16[512,512]{1,0:T(8,128)(2,1)}, u32[]{:S(2)}, u32[]{:S(2)}) collective-permute-start(bf16[512,512]{1,0:T(8,128)(2,1)} %get-tuple-element.65.rest_0_), channel_id=1, source_target_pairs={{0,3},{1,2},{2,1},{3,0},{4,7},{5,6},{6,5},{7,4},{8,11},{9,10},{10,... | collective-permute-start | bytes 1572872 | tf_op jit(solution)/shard_map/ppermute | solution.py:886
  138.8 58.6 %collective-permute-start.6 = (bf16[512,512]{1,0:T(8,128)(2,1)}, bf16[512,512]{1,0:T(8,128)(2,1)}, u32[]{:S(2)}, u32[]{:S(2)}) collective-permute-start(bf16[512,512]{1,0:T(8,128)(2,1)} %get-tuple-element.66.rest_0_), channel_id=1, source_target_pairs={{0,1},{1,0},{2,3},{3,2},{4,5},{5,4},{6,7},{7,6},{8,9},{9,8},{10,11... | collective-permute-start | bytes 1572872 | tf_op jit(solution)/shard_map/ppermute | solution.py:888
  152.4 457.6 %reduce-scatter.5.cloned.1.call-start = ((), (), s32[]{:S(2)}) async-start(), calls=%async_computation.7 | async-start | bytes 9437184 | tf_op jit(solution)/shard_map/reduce_scatter | solution.py:923
  210.0 52.7 %collective-permute-start.13 = (bf16[512,2048]{1,0:T(8,128)(2,1)}, bf16[512,2048]{1,0:T(8,128)(2,1)S(1)}, u32[]{:S(2)}, u32[]{:S(2)}) collective-permute-start(bf16[512,2048]{1,0:T(8,128)(2,1)} %get-tuple-element.71.refs_0_), channel_id=1, source_target_pairs={{0,2},{1,3},{2,0},{3,1},{4,6},{5,7},{6,4},{7,5},{8,10},{9,11},{10,... | collective-permute-start | bytes 6291464 | tf_op jit(solution)/shard_map/ppermute | solution.py:78
  220.4 45.3 %collective-permute-start.11 = (bf16[512,2048]{1,0:T(8,128)(2,1)}, bf16[512,2048]{1,0:T(8,128)(2,1)}, u32[]{:S(2)}, u32[]{:S(2)}) collective-permute-start(bf16[512,2048]{1,0:T(8,128)(2,1)} %get-tuple-element.71.refs_0_), channel_id=1, source_target_pairs={{0,1},{1,0},{2,3},{3,2},{4,5},{5,4},{6,7},{7,6},{8,9},{9,8},{10,11... | collective-permute-start | bytes 6291464 | tf_op jit(solution)/shard_map/ppermute | solution.py:78
  265.8 49.0 %collective-permute-start.15 = (bf16[512,2048]{1,0:T(8,128)(2,1)}, bf16[512,2048]{1,0:T(8,128)(2,1)}, u32[]{:S(2)}, u32[]{:S(2)}) collective-permute-start(bf16[512,2048]{1,0:T(8,128)(2,1)} %shard_map.219.refs_3_), channel_id=1, source_target_pairs={{0,1},{1,0},{2,3},{3,2},{4,5},{5,4},{6,7},{7,6},{8,9},{9,8},{10,11... | collective-permute-start | bytes 6291464 | tf_op jit(solution)/shard_map/ppermute | solution.py:78
  266.1 50.3 %collective-permute-start.16 = (bf16[512,2048]{1,0:T(8,128)(2,1)}, bf16[512,2048]{1,0:T(8,128)(2,1)}, u32[]{:S(2)}, u32[]{:S(2)}) collective-permute-start(bf16[512,2048]{1,0:T(8,128)(2,1)} %shard_map.219.refs_3_), channel_id=1, source_target_pairs={{0,2},{1,3},{2,0},{3,1},{4,6},{5,7},{6,4},{7,5},{8,10},{9,11},{10,... | collective-permute-start | bytes 6291464 | tf_op jit(solution)/shard_map/ppermute | solution.py:78
  267.4 69.7 %collective-permute-start.14 = (bf16[256,2048]{1,0:T(8,128)(2,1)S(1)}, bf16[256,2048]{1,0:T(8,128)(2,1)}, u32[]{:S(2)}, u32[]{:S(2)}) collective-permute-start(bf16[256,2048]{1,0:T(8,128)(2,1)S(1)} %shard_map.215), channel_id=1, source_target_pairs={{0,1},{1,0},{2,3},{3,2},{4,5},{5,4},{6,7},{7,6},{8,9},{9,8},{10,11... | collective-permute-start | bytes 3145736 | tf_op jit(solution)/shard_map/ppermute | solution.py:111
  271.5 65.9 %collective-permute-start.12 = (bf16[256,2048]{1,0:T(8,128)(2,1)}, bf16[256,2048]{1,0:T(8,128)(2,1)}, u32[]{:S(2)}, u32[]{:S(2)}) collective-permute-start(bf16[256,2048]{1,0:T(8,128)(2,1)} %shard_map.214), channel_id=1, source_target_pairs={{0,2},{1,3},{2,0},{3,1},{4,6},{5,7},{6,4},{7,5},{8,10},{9,11},{10,... | collective-permute-start | bytes 3145736 | tf_op jit(solution)/shard_map/ppermute | solution.py:110
  316.1 50.8 %collective-permute-start.21 = (bf16[256,2048]{1,0:T(8,128)(2,1)S(1)}, bf16[256,2048]{1,0:T(8,128)(2,1)}, u32[]{:S(2)}, u32[]{:S(2)}) collective-permute-start(bf16[256,2048]{1,0:T(8,128)(2,1)S(1)} %shard_map.220.refs_7_), channel_id=1, source_target_pairs={{0,2},{1,3},{2,0},{3,1},{4,6},{5,7},{6,4},{7,5},{8,10},{9,11},{10,... | collective-permute-start | bytes 3145736 | tf_op jit(solution)/shard_map/ppermute | solution.py:110
  317.7 50.5 %collective-permute-start.22 = (bf16[256,2048]{1,0:T(8,128)(2,1)S(1)}, bf16[256,2048]{1,0:T(8,128)(2,1)}, u32[]{:S(2)}, u32[]{:S(2)}) collective-permute-start(bf16[256,2048]{1,0:T(8,128)(2,1)S(1)} %shard_map.221.refs_8_), channel_id=1, source_target_pairs={{0,1},{1,0},{2,3},{3,2},{4,5},{5,4},{6,7},{7,6},{8,9},{9,8},{10,11... | collective-permute-start | bytes 3145736 | tf_op jit(solution)/shard_map/ppermute | solution.py:111
  397.6 284.6 %reduce-scatter.7.cloned.1.call-start = ((), (), s32[]{:S(2)}) async-start(), calls=%async_computation.8 | async-start | bytes 9437184 | tf_op jit(solution)/shard_map/reduce_scatter | solution.py:923
  492.9 254.4 %reduce-scatter.11.cloned.1.call-start = ((), (), s32[]{:S(2)}) async-start(), calls=%async_computation.10 | async-start | bytes 9437184 | tf_op jit(solution)/shard_map/reduce_scatter | solution.py:923
  561.7 228.4 %reduce-scatter.9.cloned.1.call-start = ((), (), s32[]{:S(2)}) async-start(), calls=%async_computation.9 | async-start | bytes 5898240 | tf_op jit(solution)/shard_map/reduce_scatter | solution.py:923
  603.4 87.4 %collective-permute-start.34 = (bf16[512,2048]{1,0:T(8,128)(2,1)}, bf16[512,2048]{1,0:T(8,128)(2,1)}, u32[]{:S(2)}, u32[]{:S(2)}) collective-permute-start(bf16[512,2048]{1,0:T(8,128)(2,1)} %shard_map.239.refs_3_), channel_id=1, source_target_pairs={{0,1},{1,0},{2,3},{3,2},{4,5},{5,4},{6,7},{7,6},{8,9},{9,8},{10,11... | collective-permute-start | bytes 6291464 | tf_op jit(solution)/shard_map/ppermute | solution.py:149
  603.9 86.9 %collective-permute-start.35 = (bf16[512,2048]{1,0:T(8,128)(2,1)}, bf16[512,2048]{1,0:T(8,128)(2,1)}, u32[]{:S(2)}, u32[]{:S(2)}) collective-permute-start(bf16[512,2048]{1,0:T(8,128)(2,1)} %shard_map.239.refs_3_), channel_id=1, source_target_pairs={{0,2},{1,3},{2,0},{3,1},{4,6},{5,7},{6,4},{7,5},{8,10},{9,11},{10,... | collective-permute-start | bytes 6291464 | tf_op jit(solution)/shard_map/ppermute | solution.py:149
  607.3 85.2 %collective-permute-start.36 = (bf16[512,2048]{1,0:T(8,128)(2,1)}, bf16[512,2048]{1,0:T(8,128)(2,1)}, u32[]{:S(2)}, u32[]{:S(2)}) collective-permute-start(bf16[512,2048]{1,0:T(8,128)(2,1)} %shard_map.239.refs_3_), channel_id=1, source_target_pairs={{0,3},{1,2},{2,1},{3,0},{4,7},{5,6},{6,5},{7,4},{8,11},{9,10},{10,... | collective-permute-start | bytes 6291464 | tf_op jit(solution)/shard_map/ppermute | solution.py:149
  (77 other events, 1024.7 us)
Sparse Core Ops, SparseCore 0:
  13.7 63.3 all-gather.3
  78.7 149.3 all-gather.5
  229.7 80.5 all-gather.7
  397.7 88.1 reduce-scatter.4
  493.0 88.1 reduce-scatter.6
  583.4 87.9 reduce-scatter.10
  711.6 58.8 reduce-scatter.8
where the time goes:
time: 811 us; the launch traced here: 801 us
  Pallas kernels  459 us (57%)
  waiting for transfers between devices  161 us (20%)
  starting transfers between devices  66.3 us (8%)
  local copies, waits for them, and re-layouts  52.7 us (6%)
  other arithmetic  47.3 us (6%)
  between operations  15.3 us (2%)
    pallas_call x7, Pallas kernels, back(): pl.pallas_call(functools.partial(back_kernel, count=count, terms=terms, a...  95 us
    pallas_call x4, Pallas kernels, feed(): pl.pallas_call(functools.partial(kernel, count=count), grid=(steps,), in_...  84.3 us
    ppermute x8, waiting for transfers between devices, first_hop(): return [lax.ppermute(shard, 'tensor', pairs(size, bit)) for bit in (1, 2)]  84.2 us
    pallas_call x3, Pallas kernels, weigh(): pl.pallas_call(functools.partial(weigh_kernel, count=len(lefts)), grid=(t...  76.9 us
    pallas_call x1, Pallas kernels, attend_back(): pl.pallas_call(functools.partial(attend_back_kernel, block=block), in_spe...  72.2 us
    pallas_call x4, Pallas kernels, attend(): pl.pallas_call(functools.partial(attend_kernel, block=block), in_specs=[p...  53.2 us
    unnamed x113, local copies, waits for them, and re-layouts  37.1 us
    ppermute x4, waiting for transfers between devices, second_hop(): three_b = lax.ppermute(lower, 'tensor', pairs(size, 1))  20.3 us
  transfers between devices with their start and end apart: 53, of which 14 were waited for; matrix products, arithmetic and copies ran while one was open for 9% of the time, Pallas kernels for 57%

commit v1 on v0

--- a/solution.py
+++ b/solution.py
@@ -95,6 +95,28 @@
         compiler_params=limit(52),
         cost_estimate=declared(0),
     )(value, *others)
+
+
+def add_kernel(value_ref, extra_ref, out_ref, *, which):
+    out_ref[...] = value_ref[...]
+
+    @pl.when(pl.program_id(0) == which)
+    def _():
+        out_ref[...] = (value_ref[...].astype(F32) + extra_ref[...].astype(F32)).astype(BF16)
+
+
+def add_half(value, extra, which):
+    rows, width = value.shape
+    half = pl.BlockSpec((rows // 2, width), lambda i: (i, 0))
+    return pl.pallas_call(
+        functools.partial(add_kernel, which=which),
+        grid=(2,),
+        in_specs=[half, pl.BlockSpec((rows // 2, width), lambda i: (0, 0))],
+        out_specs=half,
+        out_shape=jax.ShapeDtypeStruct((rows, width), value.dtype),
+        compiler_params=limit(52),
+        cost_estimate=declared(0),
+    )(value, extra)
 
 
 def hold_halves(hop, *others):
@@ -123,13 +145,9 @@
 
 
 def send_whole(one, two, into, size):
-    into_one, into_two = into
-    half = one.shape[0] // 2
-    lower = (one[half:].astype(F32) + into_one.astype(F32)).astype(BF16)
-    upper = (two[:half].astype(F32) + into_two.astype(F32)).astype(BF16)
     return [
-        lax.ppermute(jnp.concatenate([one[:half], lower], axis=0), "tensor", pairs(size, 1)),
-        lax.ppermute(jnp.concatenate([upper, two[half:]], axis=0), "tensor", pairs(size, 2)),
+        lax.ppermute(add_half(one, into[0], 1), "tensor", pairs(size, 1)),
+        lax.ppermute(add_half(two, into[1], 0), "tensor", pairs(size, 2)),
     ]
 
 
@@ -619,6 +637,30 @@
     )(*terms, *weights, grad, stream, gains)
 
 
+def settle_last_kernel(*refs):
+    grad_ref, x_ref, gains_ref, out_ref = refs[-4:]
+    grad_in = refs[0][...].astype(F32)
+    for term in refs[1:-4]:
+        grad_in = grad_in + term[...].astype(F32)
+    back_a = norm_back(grad_in, x_ref[...].astype(F32), gains_ref[0:1, :])
+    out_ref[...] = (grad_ref[...] + back_a).astype(BF16)
+
+
+def settle_last(terms, grad, tokens, gains):
+    rows, width = tokens.shape
+    tile = min(128, rows)
+    wide = pl.BlockSpec((tile, width), lambda i: (i, 0))
+    return pl.pallas_call(
+        settle_last_kernel,
+        grid=(rows // tile,),
+        in_specs=[wide] * (len(terms) + 2) + [pl.BlockSpec((8, width), lambda i: (0, 0))],
+        out_specs=wide,
+        out_shape=jax.ShapeDtypeStruct((rows, width), BF16),
+        compiler_params=limit(52),
+        cost_estimate=declared(rows * width),
+    )(*terms, grad, tokens, gains)
+
+
 def causal(keys, queries):
     key = lax.broadcasted_iota(jnp.int32, (keys, queries), 0)
     return key <= lax.broadcasted_iota(jnp.int32, (keys, queries), 1)
@@ -707,6 +749,28 @@
         compiler_params=limit(52),
         cost_estimate=declared(2 * 4 * HD * 4 * cells, 16),
     )(jnp.stack([bound, *order]), queries, kx, vt, *others)
+
+
+def sort_kernel(order_ref, *refs):
+    parts, out_refs = refs[:2], refs[2:]
+    block = out_refs[0].shape[0]
+    for turn, out_ref in enumerate(out_refs):
+        index = order_ref[turn]
+        rows = pl.ds(pl.multiple_of(lax.div(index, 2) * block, block), block)
+        out_ref[...] = jnp.where(lax.rem(index, 2) == 0, parts[0][rows, :], parts[1][rows, :])
+
+
+def sort_blocks(order, even, odd):
+    rows, width = even.shape[0] // 2, even.shape[1]
+    vmem = pl.BlockSpec(memory_space=pltpu.VMEM)
+    return pl.pallas_call(
+        sort_kernel,
+        in_specs=[pl.BlockSpec(memory_space=pltpu.SMEM), vmem, vmem],
+        out_specs=[vmem] * len(order),
+        out_shape=[jax.ShapeDtypeStruct((rows, width), even.dtype)] * len(order),
+        compiler_params=limit(20),
+        cost_estimate=declared(0),
+    )(jnp.stack(order), even, odd)
 
 
 def attend_back_kernel(
@@ -765,7 +829,7 @@
                         scores = dot_cols(kx_ref[group, parity, keys, :], query)
                         if diagonal:
                             scores = jnp.where(causal(size, block - skip), scores, MASKED)
-                        probs = jnp.exp(scores - lse_ref[place : place + 1, given][:, skip:])
+                        probs = jnp.exp(scores - lse_ref[place : place + 1, rows][:, skip:])
                         dprobs = dot_cols(vx_ref[group, parity, keys, :], grad)
                         delta = deltas[pair][parity : parity + 1, skip:]
                         dscores = (probs * (dprobs - delta)).astype(BF16)
@@ -874,7 +938,6 @@
 
     bound, cosine, sine = rope_tables(segment_ids)
     blocks = second_hop(inputs, hop, tensor)
-    stream = inputs.astype(F32)
     arrays = project(slots, blocks, bundle, cosine, sine, heads, kv, length)
     block_a, queries, kx, vx, kt, vt, gains = arrays
     down_t = lax.all_gather(turn(down_weight, [queries]), "dp", axis=0, tiled=True)
@@ -882,19 +945,20 @@
     if tensor == 4:
         out_own = hold(out_own, blocks[3])
         out_hop = first_hop(out_own, tensor)
-        far, far_sums = attend(bound, slots[3:], queries, kx, vt, rows)
+        odd, odd_sums = attend(bound, [jnp.int32(k) for k in (1, 3)], queries, kx, vt, rows)
+        halves = hold_halves(out_hop, odd)
+        out_all = second_hop(out_own, out_hop, tensor, halves)
+        even, even_sums = attend(bound, [jnp.int32(k) for k in (0, 2)], queries, kx, vt, rows, halves)
+        order = [slots[1], slots[2], slots[0], slots[3]]
+        first, second, own, far = sort_blocks(order, even, odd)
+        from_one = lax.ppermute(first, "tensor", pairs(tensor, 1))
+        from_two = lax.ppermute(second, "tensor", pairs(tensor, 2))
         from_far = lax.ppermute(far, "tensor", pairs(tensor, 3))
-        first, first_sums = attend(bound, slots[1:2], queries, kx, vt, rows, [far])
-        from_one = lax.ppermute(first, "tensor", pairs(tensor, 1))
-        halves = hold_halves(out_hop, first)
-        out_all = second_hop(out_own, out_hop, tensor, halves)
-        second, second_sums = attend(bound, slots[2:3], queries, kx, vt, rows, halves)
-        from_two = lax.ppermute(second, "tensor", pairs(tensor, 2))
-        own, own_sums = attend(bound, slots[:1], queries, kx, vt, rows, [second])
         stream_one, low_m = settle(own, 0, [from_one, from_two, from_far], out_all, inputs, gains)
-        order = [slots[1], slots[2], slots[0], slots[3]]
         attended = jnp.concatenate([first, second, own, far], axis=0)
-        log_sums = jnp.concatenate([first_sums, second_sums, own_sums, far_sums], axis=1)
+        log_sums = jnp.concatenate(
+            [part[:, at : at + rows] for at in (0, rows) for part in (even_sums, odd_sums)], axis=1
+        )
     else:
         order = slots
         out_all = gather(out_own, tensor)
@@ -924,13 +988,14 @@
 
     if tensor == 4:
         hop = first_hop(parts_m[0], tensor)
-        cotangent_sent = hold(cotangent, *hop)
+        fed = feed_at(3, [0], None)
+        cotangent_sent = hold(cotangent, fed[0])
         cotangent_hop = first_hop(cotangent_sent, tensor)
-        fed = feed_at(3, [0], None)
         parts_m = second_hop(parts_m[0], hop, tensor)
-        fed = feed_at(0, [1, 2], fed)
+        fed = feed_at(0, [1, 2], fed, [cotangent_sent])
         halves = hold_halves(cotangent_hop, fed[0])
         grad_parts = second_hop(cotangent_sent, cotangent_hop, tensor, halves)
+        grad_parts = grad_parts[1:] + grad_parts[:1]
         fed = feed_at(2, [3], fed, halves)
     else:
         grad_parts = second_hop(cotangent_sent, None, tensor)
@@ -939,8 +1004,6 @@
         for place in range(tensor):
             fed = feed_at(place, [place], fed)
     hidden, silu, slope, block_m = fed
-    places = [1, 2, 3, 0] if tensor == 4 else list(range(tensor))
-    grad_parts = [grad_parts[k] for k in places]
 
     def feed_back(others=()):
         return feed(
@@ -951,10 +1014,9 @@
     if tensor == 4:
         three_out = back_out([2], None, [fed[0]], True)
         out_one, out_two = out_halves = send_half(three_out, tensor)
-        down_t_wgrad = weigh(grad_parts, hidden, three_out[:1])
-        one_out, two_out, own_out = back_out(
-            [0, 1, 3], [(out_one, False), (out_two, True), None]
-        )
+        one_out, two_out, own_out = back_out([0, 1, 3], None, three_out[:1])
+        down_t_wgrad = weigh(grad_parts, hidden, [one_out])
+        one_out, two_out = add_half(one_out, out_one, 1), add_half(two_out, out_two, 0)
         out_parts = [
             own_out,
             lax.ppermute(one_out, "tensor", pairs(tensor, 1)),
@@ -993,7 +1055,7 @@
     grad_attended = jnp.concatenate([given[k] for k in places], axis=0)
     grad_qkv = attend_back(
         bound, order, queries, kx, vx, kt, log_sums, attended, grad_attended, cosine, sine, rows,
-        [down_t_low],
+        [down_t_low, layer_out],
     )
     if tensor == 4:
         sent = hold(grad_stream_low, grad_attended)
@@ -1008,18 +1070,17 @@
     if tensor == 4:
         three = back_a(slots[3:], [gate_low], True)
         halves = send_half(three, tensor)
-        block_a = hold(block_a, three[0])
+        one, two, own = back_a([slots[1], slots[2], slots[0]], three[:1])
+        block_a = hold(block_a, one)
     attention_wgrad = weigh_both(block_a, grad_qkv, grad_stream_parts, attended)
     gate_sum, up_sum, down_t_sum = [low.astype(F32) for low in (gate_low, up_low, down_t_low)]
     if tensor == 4:
         attention_wgrad = hold(attention_wgrad, *halves)
     attention_sum = reduce_rows(attention_wgrad).astype(F32)
     if tensor == 4:
-        one, two, own = back_a([slots[1], slots[2], slots[0]], three[:1])
         grad_a_parts = [own, *send_whole(one, two, halves, tensor)]
     else:
         grad_a_parts = sum_whole(back_a(slots))
-    grad_normed_a = total(grad_a_parts)
 
     product = attention_wgrad[:, :columns].astype(F32) * bundle[:, :columns].astype(F32)
     attn_term = sum_tensor(jnp.sum(product, axis=1)[None, :], tensor)
@@ -1038,7 +1099,7 @@
     mlp_term = sum_tensor(
         gain_term(mlp_gain, [(gate_weight, gate_sum), (up_weight, up_sum)])[None, :], tensor
     )
-    input_grad = (grad_stream_one + norm_back(grad_normed_a, stream, gains[0:1])).astype(BF16)
+    input_grad = settle_last(grad_a_parts, grad_stream_one, inputs, gains)
     return (
         layer_out,
         input_grad,

time: 811 us -> 801 us (0.988)
  the two profiles are of different devices: /device:TPU:26 before, /device:TPU:0 now
where the time goes in v1:
time: 801 us; the launch traced here: 795 us
  Pallas kernels  433 us (54%)
  waiting for transfers between devices  194 us (24%)
  starting transfers between devices  80.7 us (10%)
  local copies, waits for them, and re-layouts  41.1 us (5%)
  other arithmetic  31.1 us (4%)
  between operations  15 us (2%)
    pallas_call x7, Pallas kernels, back(): pl.pallas_call(functools.partial(back_kernel, count=count, terms=terms, a...  94.3 us
    pallas_call x4, Pallas kernels, feed(): pl.pallas_call(functools.partial(kernel, count=count), grid=(steps,), in_...  85.5 us
    pallas_call x3, Pallas kernels, weigh(): pl.pallas_call(functools.partial(weigh_kernel, count=len(lefts)), grid=(t...  77.3 us
    ppermute x8, waiting for transfers between devices, first_hop(): return [lax.ppermute(shard, 'tensor', pairs(size, bit)) for bit in (1, 2)]  56.2 us
    pallas_call x1, Pallas kernels, attend_back(): pl.pallas_call(functools.partial(attend_back_kernel, block=block), in_spe...  48.8 us
    ppermute x6, waiting for transfers between devices, trade(): lax.ppermute(pieces[step], 'tensor', pairs(size, step))  35.7 us
    unnamed x119, local copies, waits for them, and re-layouts  30.8 us
    pallas_call x2, Pallas kernels, attend(): pl.pallas_call(functools.partial(attend_kernel, block=block), in_specs=[p...  30 us
  transfers between devices with their start and end apart: 53, of which 23 were waited for; matrix products, arithmetic and copies ran while one was open for 5% of the time, Pallas kernels for 54%

profile of v1, /device:TPU:0, one launch (start us, length us, event | category | flops | bytes accessed | tf_op | source)
XLA Modules:
  0.0 795.0 jit_solution(15828498243028733938)
XLA Ops:
  21.3 41.0 %collective-permute-done.value_ref.refs_1_ = bf16[512,2048]{1,0:T(8,128)(2,1)S(1)} collective-permute-done((bf16[512,2048]{1,0:T(8,128)(2,1)S(1)}, bf16[512,2048]{1,0:T(8,128)(2,1)S(1)}, u32[]{:S(2)}, u32[]{:S(2)}) %collective-permute-start) | collective-permute-done | bytes 2097184 | tf_op jit(solution)/shard_map/ppermute | solution.py:78
  78.3 12.4 %collective-permute-done.2 = bf16[256,2048]{1,0:T(8,128)(2,1)S(1)} collective-permute-done((bf16[256,2048]{1,0:T(8,128)(2,1)S(1)}, bf16[256,2048]{1,0:T(8,128)(2,1)S(1)}, u32[]{:S(2)}, u32[]{:S(2)}) %collective-permute-start.2) | collective-permute-done | bytes 1048608 | tf_op jit(solution)/shard_map/ppermute | solution.py:132
  99.9 19.1 %shard_map.205 = (bf16[2048,2048]{1,0:T(8,128)(2,1)}, bf16[2048,512]{1,0:T(8,128)(2,1)}, bf16[2,2,2048,128]{3,2,1,0:T(8,128)(2,1)}, bf16[2,2,2048,128]{3,2,1,0:T...) custom-call(s32[4]{0:T(128)S(1)} %add_add_fusion.3.slot_ref, ...), custom_call_target="tpu_custom_call" | custom-call | flops 402653184 | tf_op jit(solution)/shard_map/pallas_call | solution.py:305
  123.8 18.9 %shard_map.207 = (bf16[1024,512]{1,0:T(8,128)(2,1)S(1)}, f32[8,1024]{1,0:T(8,128)S(1)}) custom-call(s32[3]{0:T(128)S(1)} %pad_add_fusion.1.order_ref, bf16[2048,512]{1,0:T(8,128)(2,1)} %get-tuple-element.62.q_ref.rest_0_, bf16[2,2,2048,128]{3,2,1,0:T(8,128)(2,1)} %get-tuple-element.63.kx_ref, bf16[128,2048]{1,0:T(8,128)(2,1)S(1)} %get-tuple-element.64.vt_ref), custom_call_target="tpu_custom_call" | custom-call | flops 343597383680 | tf_op jit(solution)/shard_map/pallas_call | solution.py:737
  209.2 23.4 %all-gather.6.cloned.1.call-done.refs_1_.refs_2_.refs_3_.refs_4_.refs_5_ = bf16[2048,4096]{1,0:T(8,128)(2,1)} async-done(((bf16[256,4096]{1,0:T(8,128)(2,1)}), bf16[2048,4096]{1,0:T(8,128)(2,1)}) %all-gather.6.cloned.1.call-update) | async-done | bytes 16777232 | tf_op jit(solution)/shard_map/all_gather | solution.py:934
  232.6 16.0 %shard_map.216 = (bf16[2048,2048]{1,0:T(8,128)(2,1)}, bf16[2048,2048]{1,0:T(8,128)(2,1)}, bf16[2048,2048]{1,0:T(8,128)(2,1)}, bf16[2048,2048]{1,0:T(8,128)(2,1)}) custom-call(bf16[512,2048]{1,0:T(8,128)(2,1)} %get-tuple-element.73.refs_0_, bf16[2048,4096]{1,0:T(8,128)(2,1)} %all-gather.6.cloned.1.call-done.refs_1_.refs_2_.refs_3_.refs_4_.refs_5_, ...), custom_call_target="tpu_custom_call" | custom-call | flops 536870912 | tf_op jit(solution)/shard_map/pallas_call | solution.py:381
  256.7 25.9 %shard_map.218 = (bf16[2048,2048]{1,0:T(8,128)(2,1)}, bf16[2048,2048]{1,0:T(8,128)(2,1)}, bf16[2048,2048]{1,0:T(8,128)(2,1)}, bf16[2048,2048]{1,0:T(8,128)(2,1)}) custom-call(bf16[512,2048]{1,0:T(8,128)(2,1)} %collective-permute-done.11.value_ref.refs_0_, ...), custom_call_target="tpu_custom_call", output_to_operand_aliasing={{0}: (4, {}), {1}: (5, {}), {2}: (6, {}), {3}: (7, {})} | custom-call | flops 1073741824 | tf_op jit(solution)/shard_map/pallas_call | solution.py:381
  282.6 14.7 %collective-permute-done.15.value_ref.refs_0_ = bf16[512,2048]{1,0:T(8,128)(2,1)S(1)} collective-permute-done((bf16[512,2048]{1,0:T(8,128)(2,1)}, bf16[512,2048]{1,0:T(8,128)(2,1)S(1)}, u32[]{:S(2)}, u32[]{:S(2)}) %collective-permute-start.15) | collective-permute-done | bytes 2097184 | tf_op jit(solution)/shard_map/ppermute | solution.py:78
  305.6 14.2 %collective-permute-done.14 = bf16[256,2048]{1,0:T(8,128)(2,1)S(1)} collective-permute-done((bf16[256,2048]{1,0:T(8,128)(2,1)S(1)}, bf16[256,2048]{1,0:T(8,128)(2,1)S(1)}, u32[]{:S(2)}, u32[]{:S(2)}) %collective-permute-start.14) | collective-permute-done | bytes 1048608 | tf_op jit(solution)/shard_map/ppermute | solution.py:133
  322.9 15.9 %shard_map.221 = (bf16[2048,2048]{1,0:T(8,128)(2,1)}, bf16[2048,2048]{1,0:T(8,128)(2,1)}, bf16[2048,2048]{1,0:T(8,128)(2,1)}, bf16[2048,2048]{1,0:T(8,128)(2,1)}) custom-call(bf16[512,2048]{1,0:T(8,128)(2,1)} %pad_maximum_fusion.refs_0_, ...), custom_call_target="tpu_custom_call", output_to_operand_aliasing={{0}: (3, {}), {1}: (4, {}), {2}: (5, {}), {3}: (6, {})} | custom-call | flops 536870912 | tf_op jit(solution)/shard_map/pallas_call | solution.py:381
  349.4 18.8 %shard_map.224 = (bf16[512,2048]{1,0:T(8,128)(2,1)}, bf16[512,2048]{1,0:T(8,128)(2,1)}, bf16[512,2048]{1,0:T(8,128)(2,1)}) custom-call(s32[3]{0:T(128)S(1)} %copy-done.22, bf16[2048,2048]{1,0:T(8,128)(2,1)} %get-tuple-element.82.refs_0_.refs_2_.refs_1_.refs_4_, bf16[2048,2048]{1,0:T(8,128)(2,1)} %get-tuple-element.82.refs_0_.refs_2_.refs_1_.refs_4_, ...), custom_call_target="tpu_custom_call" | custom-call | flops 805306368 | tf_op jit(solution)/shard_map/pallas_call | solution.py:438
  372.2 25.5 %shard_map.232.refs_0_ = bf16[2048,2048]{1,0:T(8,128)(2,1)} custom-call(bf16[512,2048]{1,0:T(8,128)(2,1)} %copy-done.27, bf16[512,2048]{1,0:T(8,128)(2,1)} %copy-done.28, bf16[512,2048]{1,0:T(8,128)(2,1)} %copy-done.31, bf16[512,2048]{1,0:T(8,128)(2,1)} %shard_map.217.refs_8_.refs_3_, bf16[2048,2048]{1,0:T(8,128)(2,1)} %get-tuple-element.82.refs_0_.refs_2_.refs_1_.refs_4_, ...), custom_call_target="tpu_custom_call" | custom-call | flops 1073741824 | tf_op jit(solution)/shard_map/pallas_call | solution.py:513
  407.2 27.7 %shard_map.227 = (bf16[2048,2048]{1,0:T(8,128)(2,1)}, bf16[2048,2048]{1,0:T(8,128)(2,1)}) custom-call(bf16[512,2048]{1,0:T(8,128)(2,1)} %copy-done.27, bf16[512,2048]{1,0:T(8,128)(2,1)} %copy-done.28, bf16[512,2048]{1,0:T(8,128)(2,1)} %copy-done.31, bf16[512,2048]{1,0:T(8,128)(2,1)} %shard_map.217.refs_8_.refs_3_, ...), custom_call_target="tpu_custom_call" | custom-call | flops 1073741824 | tf_op jit(solution)/shard_map/pallas_call | solution.py:381
  434.9 13.9 %shard_map.228 = (bf16[256,2048]{1,0:T(8,128)(2,1)S(1)}, bf16[256,2048]{1,0:T(8,128)(2,1)}) custom-call(s32[1]{0:T(128)} %constant.52.clone.1.slot_ref, bf16[2048,2048]{1,0:T(8,128)(2,1)} %get-tuple-element.94.refs_0_.refs_2_.refs_1_, bf16[2048,2048]{1,0:T(8,128)(2,1)} %get-tuple-element.95.refs_1_.refs_3_, ...), custom_call_target="tpu_custom_call" | custom-call | flops 536870912 | tf_op jit(solution)/shard_map/pallas_call | solution.py:438
  453.3 26.3 %shard_map.235.refs_0_ = bf16[2048,2048]{1,0:T(8,128)(2,1)} custom-call(bf16[2048,2048]{1,0:T(8,128)(2,1)} %get-tuple-element.104.refs_0_, bf16[2048,2048]{1,0:T(8,128)(2,1)} %get-tuple-element.94.refs_0_.refs_2_.refs_1_, bf16[256,2048]{1,0:T(8,128)(2,1)S(1)} %get-tuple-element.97.refs_2_, bf16[512,2048]{1,0:T(8,128)(2,1)} %copy-done.36, ...), custom_call_target="tpu_custom_call" | custom-call | flops 1073741824 | tf_op jit(solution)/shard_map/pallas_call | solution.py:513
  482.8 24.7 %shard_map.229 = (bf16[512,2048]{1,0:T(8,128)(2,1)}, bf16[512,2048]{1,0:T(8,128)(2,1)}) custom-call(s32[2]{0:T(128)S(1)} %iota.41.slot_ref, bf16[2048,2048]{1,0:T(8,128)(2,1)} %get-tuple-element.94.refs_0_.refs_2_.refs_1_, bf16[2048,2048]{1,0:T(8,128)(2,1)} %get-tuple-element.95.refs_1_.refs_3_, ...), custom_call_target="tpu_custom_call" | custom-call | flops 1073741824 | tf_op jit(solution)/shard_map/pallas_call | solution.py:438
  512.1 14.0 %shard_map.230.refs_0_.refs_2_ = bf16[512,2048]{1,0:T(8,128)(2,1)} custom-call(s32[1]{0:T(128)} %constant.60.clone.1.slot_ref, bf16[2048,2048]{1,0:T(8,128)(2,1)} %get-tuple-element.94.refs_0_.refs_2_.refs_1_, bf16[2048,2048]{1,0:T(8,128)(2,1)} %get-tuple-element.95.refs_1_.refs_3_, ...), custom_call_target="tpu_custom_call" | custom-call | flops 536870912 | tf_op jit(solution)/shard_map/pallas_call | solution.py:438
  526.0 25.5 %shard_map.246.refs_0_ = bf16[2048,2048]{1,0:T(8,128)(2,1)} custom-call(bf16[2048,2048]{1,0:T(8,128)(2,1)} %get-tuple-element.104.refs_0_, bf16[2048,2048]{1,0:T(8,128)(2,1)} %get-tuple-element.95.refs_1_.refs_3_, bf16[512,2048]{1,0:T(8,128)(2,1)} %shard_map.230.refs_0_.refs_2_), custom_call_target="tpu_custom_call" | custom-call | flops 1073741824 | tf_op jit(solution)/shard_map/pallas_call | solution.py:513
  553.7 13.8 %shard_map.231 = (f32[512,2048]{1,0:T(8,128)}, bf16[512,2048]{1,0:T(8,128)(2,1)}, bf16[512,512]{1,0:T(8,128)(2,1)S(1)}, bf16[512,512]{1,0:T(8,128)(2,1)S(1)}, bf...) custom-call(bf16[512,2048]{1,0:T(8,128)(2,1)} %shard_map.230.refs_0_.refs_2_, bf16[512,2048]{1,0:T(8,128)(2,1)} %copy-done.32, ...), custom_call_target="tpu_custom_call" | custom-call | flops 268435456 | tf_op jit(solution)/shard_map/pallas_call | solution.py:623
  602.4 48.8 %shard_map.234.refs_0_.refs_1_.refs_2_.refs_5_ = bf16[2048,768]{1,0:T(8,128)(2,1)} custom-call(s32[5]{0:T(128)S(1)} %stack.69.order_ref, bf16[2048,512]{1,0:T(8,128)(2,1)} %get-tuple-element.62.q_ref.rest_0_, bf16[2,2,2048,128]{3,2,1,0:T(8,128)(2,1)} %get-tuple-element.63.kx_ref, bf16[2,2,2048,128]{3,2,1,0:T(8,128)(2,1)} %get-tuple-element.88.vx_ref, ...), custom_call_target="tpu_custom_call" | custom-call | flops 6710886400 | tf_op jit(solution)/shard_map/pallas_call | solution.py:887
  672.1 14.4 %collective-permute-done.36.refs_4_ = bf16[512,2048]{1,0:T(8,128)(2,1)} collective-permute-done((bf16[512,2048]{1,0:T(8,128)(2,1)}, bf16[512,2048]{1,0:T(8,128)(2,1)}, u32[]{:S(2)}, u32[]{:S(2)}) %collective-permute-start.36) | collective-permute-done | bytes 2097184 | tf_op jit(solution)/shard_map/ppermute | solution.py:167
  686.5 17.0 %shard_map.244.refs_0_ = bf16[2048,1280]{1,0:T(8,128)(2,1)} custom-call(bf16[2048,2048]{1,0:T(8,128)(2,1)} %shard_map.242.refs_0_, bf16[512,2048]{1,0:T(8,128)(2,1)} %collective-permute-done.34.refs_1_, bf16[512,2048]{1,0:T(8,128)(2,1)} %collective-permute-done.35.refs_2_, bf16[512,2048]{1,0:T(8,128)(2,1)} %shard_map.243.refs_3_, ...), custom_call_target="tpu_custom_call" | custom-call | flops 671088640 | tf_op jit(solution)/shard_map/pallas_call | solution.py:544
  741.7 17.9 %collective-permute-done.45 = f32[1,256]{1,0:T(1,128)S(1)} collective-permute-done((f32[1,256]{1,0:T(1,128)S(1)}, f32[1,256]{1,0:T(1,128)S(1)}, u32[]{:S(2)}, u32[]{:S(2)}) %collective-permute-start.45) | collective-permute-done | bytes 1056 | tf_op jit(solution)/shard_map/ppermute | solution.py:178
  759.5 14.9 %collective-permute-start.42 = (f32[1,2048]{1,0:T(1,128)S(1)}, f32[1,2048]{1,0:T(1,128)S(1)}, u32[]{:S(2)}, u32[]{:S(2)}) collective-permute-start(f32[1,2048]{1,0:T(1,128)S(1)} %add.73), channel_id=1, source_target_pairs={{0,16},{4,20},{8,24},{12,28},{16,0},{20,4},{24,8},{28,12},{1,17},{... | collective-permute-start | bytes 24584 | tf_op jit(solution)/shard_map/ppermute | solution.py:186
  (298 shorter events, 275.6 us)
Async XLA Ops:
  7.2 86.8 %all-gather.4.cloned.1.call-start = ((), (), s32[]{:S(2)}) async-start(), calls=%async_computation.4 | async-start | bytes 7077888 | tf_op jit(solution)/shard_map/all_gather | solution.py:928
  13.6 219.0 %all-gather.6.cloned.1.call-start = ((), (), s32[]{:S(2)}) async-start(), calls=%async_computation.5 | async-start | bytes 18874368 | tf_op jit(solution)/shard_map/all_gather | solution.py:934
  13.7 48.6 %collective-permute-start = (bf16[512,2048]{1,0:T(8,128)(2,1)S(1)}, bf16[512,2048]{1,0:T(8,128)(2,1)S(1)}, u32[]{:S(2)}, u32[]{:S(2)}) collective-permute-start(bf16[512,2048]{1,0:T(8,128)(2,1)S(1)} %copy-done.25), channel_id=1, source_target_pairs={{0,1},{1,0},{2,3},{3,2},{4,5},{5,4},{6,7},{7,6},{8,9},{9,8},{10,11... | collective-permute-start | bytes 6291464 | tf_op jit(solution)/shard_map/ppermute | solution.py:78
  16.7 47.2 %collective-permute-start.1 = (bf16[512,2048]{1,0:T(8,128)(2,1)S(1)}, bf16[512,2048]{1,0:T(8,128)(2,1)}, u32[]{:S(2)}, u32[]{:S(2)}) collective-permute-start(bf16[512,2048]{1,0:T(8,128)(2,1)S(1)} %copy-done.25), channel_id=1, source_target_pairs={{0,2},{1,3},{2,0},{3,1},{4,6},{5,7},{6,4},{7,5},{8,10},{9,11},{10,... | collective-permute-start | bytes 6291464 | tf_op jit(solution)/shard_map/ppermute | solution.py:78
  63.9 274.8 %all-gather.8.cloned.1.call-start = ((), (), s32[]{:S(2)}) async-start(), calls=%async_computation.6 | async-start | bytes 9437184 | tf_op jit(solution)/shard_map/all_gather | solution.py:943
  99.3 47.9 %collective-permute-start.5 = (bf16[2048,512]{1,0:T(8,128)(2,1)}, bf16[2048,512]{1,0:T(8,128)(2,1)}, u32[]{:S(2)}, u32[]{:S(2)}) collective-permute-start(bf16[2048,512]{1,0:T(8,128)(2,1)} %shard_map.206.refs_4_.refs_3_), channel_id=1, source_target_pairs={{0,2},{1,3},{2,0},{3,1},{4,6},{5,7},{6,4},{7,5},{8,10},{9,11},{10,... | collective-permute-start | bytes 6291464 | tf_op jit(solution)/shard_map/ppermute | solution.py:78
  123.5 478.9 %reduce-scatter.5.cloned.1.call-start = ((), (), s32[]{:S(2)}) async-start(), calls=%async_computation.7 | async-start | bytes 9437184 | tf_op jit(solution)/shard_map/reduce_scatter | solution.py:987
  248.6 48.7 %collective-permute-start.15 = (bf16[512,2048]{1,0:T(8,128)(2,1)}, bf16[512,2048]{1,0:T(8,128)(2,1)S(1)}, u32[]{:S(2)}, u32[]{:S(2)}) collective-permute-start(bf16[512,2048]{1,0:T(8,128)(2,1)} %shard_map.217.refs_8_.refs_3_), channel_id=1, source_target_pairs={{0,1},{1,0},{2,3},{3,2},{4,5},{5,4},{6,7},{7,6},{8,9},{9,8},{10,11... | collective-permute-start | bytes 6291464 | tf_op jit(solution)/shard_map/ppermute | solution.py:78
  250.1 51.3 %collective-permute-start.16 = (bf16[512,2048]{1,0:T(8,128)(2,1)}, bf16[512,2048]{1,0:T(8,128)(2,1)S(1)}, u32[]{:S(2)}, u32[]{:S(2)}) collective-permute-start(bf16[512,2048]{1,0:T(8,128)(2,1)} %shard_map.217.refs_8_.refs_3_), channel_id=1, source_target_pairs={{0,2},{1,3},{2,0},{3,1},{4,6},{5,7},{6,4},{7,5},{8,10},{9,11},{10,... | collective-permute-start | bytes 6291464 | tf_op jit(solution)/shard_map/ppermute | solution.py:78
  254.2 65.5 %collective-permute-start.14 = (bf16[256,2048]{1,0:T(8,128)(2,1)S(1)}, bf16[256,2048]{1,0:T(8,128)(2,1)S(1)}, u32[]{:S(2)}, u32[]{:S(2)}) collective-permute-start(bf16[256,2048]{1,0:T(8,128)(2,1)S(1)} %shard_map.214), channel_id=1, source_target_pairs={{0,1},{1,0},{2,3},{3,2},{4,5},{5,4},{6,7},{7,6},{8,9},{9,8},{10,11... | collective-permute-start | bytes 3145736 | tf_op jit(solution)/shard_map/ppermute | solution.py:133
  256.1 65.2 %collective-permute-start.12 = (bf16[256,2048]{1,0:T(8,128)(2,1)S(1)}, bf16[256,2048]{1,0:T(8,128)(2,1)S(1)}, u32[]{:S(2)}, u32[]{:S(2)}) collective-permute-start(bf16[256,2048]{1,0:T(8,128)(2,1)S(1)} %shard_map.213), channel_id=1, source_target_pairs={{0,2},{1,3},{2,0},{3,1},{4,6},{5,7},{6,4},{7,5},{8,10},{9,11},{10,... | collective-permute-start | bytes 3145736 | tf_op jit(solution)/shard_map/ppermute | solution.py:132
  299.8 68.4 %collective-permute-start.21 = (bf16[256,2048]{1,0:T(8,128)(2,1)S(1)}, bf16[256,2048]{1,0:T(8,128)(2,1)}, u32[]{:S(2)}, u32[]{:S(2)}) collective-permute-start(bf16[256,2048]{1,0:T(8,128)(2,1)S(1)} %shard_map.219.refs_7_), channel_id=1, source_target_pairs={{0,2},{1,3},{2,0},{3,1},{4,6},{5,7},{6,4},{7,5},{8,10},{9,11},{10,... | collective-permute-start | bytes 3145736 | tf_op jit(solution)/shard_map/ppermute | solution.py:132
  304.0 65.5 %collective-permute-start.22 = (bf16[256,2048]{1,0:T(8,128)(2,1)S(1)}, bf16[256,2048]{1,0:T(8,128)(2,1)}, u32[]{:S(2)}, u32[]{:S(2)}) collective-permute-start(bf16[256,2048]{1,0:T(8,128)(2,1)S(1)} %shard_map.220.refs_8_), channel_id=1, source_target_pairs={{0,1},{1,0},{2,3},{3,2},{4,5},{5,4},{6,7},{7,6},{8,9},{9,8},{10,11... | collective-permute-start | bytes 3145736 | tf_op jit(solution)/shard_map/ppermute | solution.py:133
  347.4 50.4 %collective-permute-start.19 = (bf16[256,2048]{1,0:T(8,128)(2,1)S(1)}, bf16[256,2048]{1,0:T(8,128)(2,1)}, u32[]{:S(2)}, u32[]{:S(2)}) collective-permute-start(bf16[256,2048]{1,0:T(8,128)(2,1)S(1)} %get-tuple-element.83.refs_4_), channel_id=1, source_target_pairs={{0,1},{1,0},{2,3},{3,2},{4,5},{5,4},{6,7},{7,6},{8,9},{9,8},{10,11... | collective-permute-start | bytes 3145736 | tf_op jit(solution)/shard_map/ppermute | solution.py:142
  347.9 49.9 %collective-permute-start.17 = (bf16[256,2048]{1,0:T(8,128)(2,1)}, bf16[256,2048]{1,0:T(8,128)(2,1)S(1)}, u32[]{:S(2)}, u32[]{:S(2)}) collective-permute-start(bf16[256,2048]{1,0:T(8,128)(2,1)} %get-tuple-element.86), channel_id=1, source_target_pairs={{0,2},{1,3},{2,0},{3,1},{4,6},{5,7},{6,4},{7,5},{8,10},{9,11},{10,... | collective-permute-start | bytes 3145736 | tf_op jit(solution)/shard_map/ppermute | solution.py:143
  398.8 252.4 %reduce-scatter.7.cloned.1.call-start = ((), (), s32[]{:S(2)}) async-start(), calls=%async_computation.8 | async-start | bytes 9437184 | tf_op jit(solution)/shard_map/reduce_scatter | solution.py:987
  402.3 48.6 %collective-permute-start.20 = (bf16[512,2048]{1,0:T(8,128)(2,1)}, bf16[512,2048]{1,0:T(8,128)(2,1)S(1)}, u32[]{:S(2)}, u32[]{:S(2)}) collective-permute-start(bf16[512,2048]{1,0:T(8,128)(2,1)} %shard_map.226), channel_id=1, source_target_pairs={{0,2},{1,3},{2,0},{3,1},{4,6},{5,7},{6,4},{7,5},{8,10},{9,11},{10,... | collective-permute-start | bytes 6291464 | tf_op jit(solution)/shard_map/ppermute | solution.py:1023
  481.6 241.4 %reduce-scatter.11.cloned.1.call-start = ((), (), s32[]{:S(2)}) async-start(), calls=%async_computation.10 | async-start | bytes 9437184 | tf_op jit(solution)/shard_map/reduce_scatter | solution.py:987
  552.9 231.2 %reduce-scatter.9.cloned.1.call-start = ((), (), s32[]{:S(2)}) async-start(), calls=%async_computation.9 | async-start | bytes 5898240 | tf_op jit(solution)/shard_map/reduce_scatter | solution.py:987
  591.3 77.9 %collective-permute-start.34 = (bf16[512,2048]{1,0:T(8,128)(2,1)}, bf16[512,2048]{1,0:T(8,128)(2,1)}, u32[]{:S(2)}, u32[]{:S(2)}) collective-permute-start(bf16[512,2048]{1,0:T(8,128)(2,1)} %shard_map.243.refs_3_), channel_id=1, source_target_pairs={{0,1},{1,0},{2,3},{3,2},{4,5},{5,4},{6,7},{7,6},{8,9},{9,8},{10,11... | collective-permute-start | bytes 6291464 | tf_op jit(solution)/shard_map/ppermute | solution.py:167
  591.3 80.8 %collective-permute-start.35 = (bf16[512,2048]{1,0:T(8,128)(2,1)}, bf16[512,2048]{1,0:T(8,128)(2,1)}, u32[]{:S(2)}, u32[]{:S(2)}) collective-permute-start(bf16[512,2048]{1,0:T(8,128)(2,1)} %shard_map.243.refs_3_), channel_id=1, source_target_pairs={{0,2},{1,3},{2,0},{3,1},{4,6},{5,7},{6,4},{7,5},{8,10},{9,11},{10,... | collective-permute-start | bytes 6291464 | tf_op jit(solution)/shard_map/ppermute | solution.py:167
  595.2 91.3 %collective-permute-start.36 = (bf16[512,2048]{1,0:T(8,128)(2,1)}, bf16[512,2048]{1,0:T(8,128)(2,1)}, u32[]{:S(2)}, u32[]{:S(2)}) collective-permute-start(bf16[512,2048]{1,0:T(8,128)(2,1)} %shard_map.243.refs_3_), channel_id=1, source_target_pairs={{0,3},{1,2},{2,1},{3,0},{4,7},{5,6},{6,5},{7,4},{8,11},{9,10},{10,... | collective-permute-start | bytes 6291464 | tf_op jit(solution)/shard_map/ppermute | solution.py:167
  715.7 60.9 %collective-permute-start.31 = (bf16[512,2048]{1,0:T(8,128)(2,1)}, bf16[512,2048]{1,0:T(8,128)(2,1)}, u32[]{:S(2)}, u32[]{:S(2)}) collective-permute-start(bf16[512,2048]{1,0:T(8,128)(2,1)} %shard_map.239), channel_id=1, source_target_pairs={{0,1},{1,0},{2,3},{3,2},{4,5},{5,4},{6,7},{7,6},{8,9},{9,8},{10,11... | collective-permute-start | bytes 6291464 | tf_op jit(solution)/shard_map/ppermute | solution.py:149
  721.1 55.5 %collective-permute-start.33 = (bf16[512,2048]{1,0:T(8,128)(2,1)}, bf16[512,2048]{1,0:T(8,128)(2,1)}, u32[]{:S(2)}, u32[]{:S(2)}) collective-permute-start(bf16[512,2048]{1,0:T(8,128)(2,1)} %shard_map.240), channel_id=1, source_target_pairs={{0,2},{1,3},{2,0},{3,1},{4,6},{5,7},{6,4},{7,5},{8,10},{9,11},{10,... | collective-permute-start | bytes 6291464 | tf_op jit(solution)/shard_map/ppermute | solution.py:150
  (80 other events, 1253.1 us)
Sparse Core Ops, SparseCore 0:
  13.7 67.4 all-gather.3
  82.8 149.7 all-gather.5
  234.2 80.2 all-gather.7
  398.9 92.9 reduce-scatter.4
  494.1 87.9 reduce-scatter.6
  584.2 87.9 reduce-scatter.10
  705.6 67.2 reduce-scatter.8

commit v2 on v1

--- a/solution.py
+++ b/solution.py
@@ -142,13 +142,6 @@
     into_two = lax.ppermute(three[0], "tensor", pairs(size, 1))
     into_one = lax.ppermute(three[1], "tensor", pairs(size, 2))
     return into_one, into_two
-
-
-def send_whole(one, two, into, size):
-    return [
-        lax.ppermute(add_half(one, into[0], 1), "tensor", pairs(size, 1)),
-        lax.ppermute(add_half(two, into[1], 0), "tensor", pairs(size, 2)),
-    ]
 
 
 def sum_whole(terms):
@@ -661,6 +654,27 @@
     )(*terms, grad, tokens, gains)
 
 
+def finish_kernel(*refs, count):
+    value = refs[count][...]
+    for term in refs[:count]:
+        value = value + term[...].astype(F32)
+    refs[-1][...] = value.astype(BF16)
+
+
+def finish(terms, stream, others=()):
+    rows, width = stream.shape
+    wide = pl.BlockSpec((rows // 4, width), lambda i: (i, 0))
+    return pl.pallas_call(
+        functools.partial(finish_kernel, count=len(terms)),
+        grid=(4,),
+        in_specs=[wide] * (len(terms) + 1) + [ANYWHERE] * len(others),
+        out_specs=wide,
+        out_shape=jax.ShapeDtypeStruct((rows, width), BF16),
+        compiler_params=limit(52),
+        cost_estimate=declared(rows * width),
+    )(*terms, stream, *others)
+
+
 def causal(keys, queries):
     key = lax.broadcasted_iota(jnp.int32, (keys, queries), 0)
     return key <= lax.broadcasted_iota(jnp.int32, (keys, queries), 1)
@@ -954,7 +968,11 @@
         from_one = lax.ppermute(first, "tensor", pairs(tensor, 1))
         from_two = lax.ppermute(second, "tensor", pairs(tensor, 2))
         from_far = lax.ppermute(far, "tensor", pairs(tensor, 3))
-        stream_one, low_m = settle(own, 0, [from_one, from_two, from_far], out_all, inputs, gains)
+        cotangent_sent = hold(cotangent, first, out_all[3])
+        cotangent_hop = first_hop(cotangent_sent, tensor)
+        stream_one, low_m = settle(
+            own, 0, [from_one, from_two, from_far], out_all, inputs, gains, [cotangent_sent]
+        )
         attended = jnp.concatenate([first, second, own, far], axis=0)
         log_sums = jnp.concatenate(
             [part[:, at : at + rows] for at in (0, rows) for part in (even_sums, odd_sums)], axis=1
@@ -987,12 +1005,11 @@
         return lax.psum_scatter(term, "dp", scatter_dimension=0, tiled=True)
 
     if tensor == 4:
-        hop = first_hop(parts_m[0], tensor)
         fed = feed_at(3, [0], None)
-        cotangent_sent = hold(cotangent, fed[0])
-        cotangent_hop = first_hop(cotangent_sent, tensor)
-        parts_m = second_hop(parts_m[0], hop, tensor)
-        fed = feed_at(0, [1, 2], fed, [cotangent_sent])
+        sent = hold(parts_m[0], fed[0], *cotangent_hop)
+        hop = first_hop(sent, tensor)
+        parts_m = second_hop(sent, hop, tensor)
+        fed = feed_at(0, [1, 2], fed, [sent])
         halves = hold_halves(cotangent_hop, fed[0])
         grad_parts = second_hop(cotangent_sent, cotangent_hop, tensor, halves)
         grad_parts = grad_parts[1:] + grad_parts[:1]
@@ -1014,9 +1031,8 @@
     if tensor == 4:
         three_out = back_out([2], None, [fed[0]], True)
         out_one, out_two = out_halves = send_half(three_out, tensor)
-        one_out, two_out, own_out = back_out([0, 1, 3], None, three_out[:1])
-        down_t_wgrad = weigh(grad_parts, hidden, [one_out])
-        one_out, two_out = add_half(one_out, out_one, 1), add_half(two_out, out_two, 0)
+        down_t_wgrad = weigh(grad_parts, hidden, three_out[:1])
+        one_out, two_out, own_out = back_out([0, 1, 3], [(out_one, False), (out_two, True), None])
         out_parts = [
             own_out,
             lax.ppermute(one_out, "tensor", pairs(tensor, 1)),
@@ -1040,7 +1056,6 @@
         grad_m_parts = sum_whole(back_m(list(range(tensor)), fed))
         gate_wgrad, up_wgrad = weigh([block_m], fed[0]), weigh([block_m], fed[1])
         out_parts = sum_whole(back_out(list(range(tensor))))
-    layer_out = (stream_one + total(out_parts)).astype(BF16)
     if tensor != 4:
         out_halves = m_halves = ()
     down_t_low = reduce_rows(down_t_wgrad, *out_halves)
@@ -1055,7 +1070,7 @@
     grad_attended = jnp.concatenate([given[k] for k in places], axis=0)
     grad_qkv = attend_back(
         bound, order, queries, kx, vx, kt, log_sums, attended, grad_attended, cosine, sine, rows,
-        [down_t_low, layer_out],
+        [down_t_low],
     )
     if tensor == 4:
         sent = hold(grad_stream_low, grad_attended)
@@ -1070,7 +1085,7 @@
     if tensor == 4:
         three = back_a(slots[3:], [gate_low], True)
         halves = send_half(three, tensor)
-        one, two, own = back_a([slots[1], slots[2], slots[0]], three[:1])
+        one, two = back_a([slots[1], slots[2]], three[:1])
         block_a = hold(block_a, one)
     attention_wgrad = weigh_both(block_a, grad_qkv, grad_stream_parts, attended)
     gate_sum, up_sum, down_t_sum = [low.astype(F32) for low in (gate_low, up_low, down_t_low)]
@@ -1078,9 +1093,16 @@
         attention_wgrad = hold(attention_wgrad, *halves)
     attention_sum = reduce_rows(attention_wgrad).astype(F32)
     if tensor == 4:
-        grad_a_parts = [own, *send_whole(one, two, halves, tensor)]
+        one, two = add_half(one, halves[0], 1), add_half(two, halves[1], 0)
+        sent = [
+            lax.ppermute(one, "tensor", pairs(tensor, 1)),
+            lax.ppermute(two, "tensor", pairs(tensor, 2)),
+        ]
+        grad_a_parts = [*back_a([slots[0]], [one, two]), *sent]
+        layer_out = finish(out_parts, stream_one, grad_a_parts[:1])
     else:
         grad_a_parts = sum_whole(back_a(slots))
+        layer_out = finish(out_parts, stream_one)
 
     product = attention_wgrad[:, :columns].astype(F32) * bundle[:, :columns].astype(F32)
     attn_term = sum_tensor(jnp.sum(product, axis=1)[None, :], tensor)

time: 801 us -> 846 us (1.056); the launches traced: 795 us -> 851 us
  Pallas kernels: 433 us -> 475 us
  starting transfers between devices: 80.7 us -> 102 us
  waiting for transfers between devices: 194 us -> 185 us
  local copies, waits for them, and re-layouts: 41.1 us -> 49.6 us
    ppermute x1, waiting for transfers between devices: 9.78 us -> 42 us  [local(): from_one = lax.ppermute(first, 'tensor', pairs(tensor, 1))]
    pallas_call x1, Pallas kernels: 48.8 us -> 72.2 us  [attend_back(): pl.pallas_call(functools.partial(attend_back_kernel, block=block), in_spe...]
    all_gather x1, waiting for transfers between devices: 23.4 us -> 0.01 us  [local(): lax.all_gather(hold(jnp.concatenate([gate_weight, up_weight], axis=1), *(...]
    ppermute x8, waiting for transfers between devices: 56.2 us -> 78.9 us  [first_hop(): return [lax.ppermute(shard, 'tensor', pairs(size, bit)) for bit in (1, 2)]]
    ppermute x6, starting transfers between devices: 7.57 us -> 23.8 us  [trade(): lax.ppermute(pieces[step], 'tensor', pairs(size, step))]
    ppermute x4, waiting for transfers between devices: 19.3 us -> 3.07 us  [second_hop(): three_b = lax.ppermute(lower, 'tensor', pairs(size, 1))]
    pallas_call x2, Pallas kernels: 30 us -> 46.2 us  [attend(): pl.pallas_call(functools.partial(attend_kernel, block=block), in_specs=[p...]
    ppermute x6, waiting for transfers between devices: 35.7 us -> 21.6 us  [trade(): lax.ppermute(pieces[step], 'tensor', pairs(size, step))]
  transfers between devices with their start and end apart: 53 -> 53, of which waited for: 23 -> 13; matrix products, arithmetic and copies ran while one was open for 5% -> 4% of each run, Pallas kernels for 54% -> 56%
where the time goes in v2:
time: 846 us; the launch traced here: 851 us
  Pallas kernels  475 us (56%)
  waiting for transfers between devices  185 us (22%)
  starting transfers between devices  102 us (12%)
  local copies, waits for them, and re-layouts  49.6 us (6%)
  other arithmetic  23.9 us (3%)
  between operations  15 us (2%)
    pallas_call x8, Pallas kernels, back(): pl.pallas_call(functools.partial(back_kernel, count=count, terms=terms, a...  98.7 us
    pallas_call x4, Pallas kernels, feed(): pl.pallas_call(functools.partial(kernel, count=count), grid=(steps,), in_...  84.5 us
    ppermute x8, waiting for transfers between devices, first_hop(): return [lax.ppermute(shard, 'tensor', pairs(size, bit)) for bit in (1, 2)]  78.9 us
    pallas_call x3, Pallas kernels, weigh(): pl.pallas_call(functools.partial(weigh_kernel, count=len(lefts)), grid=(t...  77.1 us
    pallas_call x1, Pallas kernels, attend_back(): pl.pallas_call(functools.partial(attend_back_kernel, block=block), in_spe...  72.2 us
    pallas_call x2, Pallas kernels, attend(): pl.pallas_call(functools.partial(attend_kernel, block=block), in_specs=[p...  46.2 us
    ppermute x1, waiting for transfers between devices, local(): from_one = lax.ppermute(first, 'tensor', pairs(tensor, 1))  42 us
    unnamed x119, local copies, waits for them, and re-layouts  38.5 us
  transfers between devices with their start and end apart: 53, of which 13 were waited for; matrix products, arithmetic and copies ran while one was open for 4% of the time, Pallas kernels for 56%

profile of v2, /device:TPU:0, one launch (start us, length us, event | category | flops | bytes accessed | tf_op | source)
XLA Modules:
  0.0 850.8 jit_solution(6591376802602290772)
XLA Ops:
  21.3 41.0 %collective-permute-done.value_ref.refs_1_ = bf16[512,2048]{1,0:T(8,128)(2,1)S(1)} collective-permute-done((bf16[512,2048]{1,0:T(8,128)(2,1)S(1)}, bf16[512,2048]{1,0:T(8,128)(2,1)S(1)}, u32[]{:S(2)}, u32[]{:S(2)}) %collective-permute-start) | collective-permute-done | bytes 2097184 | tf_op jit(solution)/shard_map/ppermute | solution.py:78
  80.8 12.4 %collective-permute-done.2 = bf16[256,2048]{1,0:T(8,128)(2,1)S(1)} collective-permute-done((bf16[256,2048]{1,0:T(8,128)(2,1)S(1)}, bf16[256,2048]{1,0:T(8,128)(2,1)S(1)}, u32[]{:S(2)}, u32[]{:S(2)}) %collective-permute-start.2) | collective-permute-done | bytes 1048608 | tf_op jit(solution)/shard_map/ppermute | solution.py:132
  102.3 19.0 %shard_map.205 = (bf16[2048,2048]{1,0:T(8,128)(2,1)}, bf16[2048,512]{1,0:T(8,128)(2,1)}, bf16[2,2,2048,128]{3,2,1,0:T(8,128)(2,1)}, bf16[2,2,2048,128]{3,2,1,0:T...) custom-call(s32[4]{0:T(128)S(1)} %add_add_fusion.3.slot_ref, ...), custom_call_target="tpu_custom_call" | custom-call | flops 402653184 | tf_op jit(solution)/shard_map/pallas_call | solution.py:298
  126.4 27.1 %shard_map.207 = (bf16[1024,512]{1,0:T(8,128)(2,1)S(1)}, f32[8,1024]{1,0:T(8,128)S(1)}) custom-call(s32[3]{0:T(128)S(1)} %pad_add_fusion.1.order_ref, bf16[2048,512]{1,0:T(8,128)(2,1)} %get-tuple-element.61.q_ref.rest_0_, bf16[2,2,2048,128]{3,2,1,0:T(8,128)(2,1)} %get-tuple-element.62.kx_ref, bf16[128,2048]{1,0:T(8,128)(2,1)S(1)} %get-tuple-element.63.vt_ref), custom_call_target="tpu_custom_call" | custom-call | flops 343597383680 | tf_op jit(solution)/shard_map/pallas_call | solution.py:751
  160.7 19.1 %shard_map.210 = (bf16[1024,512]{1,0:T(8,128)(2,1)S(1)}, f32[8,1024]{1,0:T(8,128)S(1)}) custom-call(s32[3]{0:T(128)S(1)} %pad_add_fusion.order_ref, bf16[2048,512]{1,0:T(8,128)(2,1)} %get-tuple-element.61.q_ref.rest_0_, bf16[2,2,2048,128]{3,2,1,0:T(8,128)(2,1)} %get-tuple-element.62.kx_ref, bf16[128,2048]{1,0:T(8,128)(2,1)S(1)} %get-tuple-element.63.vt_ref, ...), custom_call_target="tpu_custom_call" | custom-call | flops 343597383680 | tf_op jit(solution)/shard_map/pallas_call | solution.py:751
  191.3 42.0 %collective-permute-done.6.refs_1_ = bf16[512,512]{1,0:T(8,128)(2,1)S(1)} collective-permute-done((bf16[512,512]{1,0:T(8,128)(2,1)S(1)}, bf16[512,512]{1,0:T(8,128)(2,1)S(1)}, u32[]{:S(2)}, u32[]{:S(2)}) %collective-permute-start.6) | collective-permute-done | bytes 524320 | tf_op jit(solution)/shard_map/ppermute | solution.py:968
  253.0 15.8 %shard_map.215 = (bf16[2048,2048]{1,0:T(8,128)(2,1)}, bf16[2048,2048]{1,0:T(8,128)(2,1)}, bf16[2048,2048]{1,0:T(8,128)(2,1)}, bf16[2048,2048]{1,0:T(8,128)(2,1)}) custom-call(bf16[512,2048]{1,0:T(8,128)(2,1)} %get-tuple-element.71.refs_0_, bf16[2048,4096]{1,0:T(8,128)(2,1)} %all-gather.6.cloned.1.call-done.refs_1_.refs_2_.refs_3_.refs_4_.refs_5_, ...), custom_call_target="tpu_custom_call" | custom-call | flops 536870912 | tf_op jit(solution)/shard_map/pallas_call | solution.py:374
  271.9 37.6 %collective-permute-done.13.value_ref.refs_0_ = bf16[512,2048]{1,0:T(8,128)(2,1)S(1)} collective-permute-done((bf16[512,2048]{1,0:T(8,128)(2,1)}, bf16[512,2048]{1,0:T(8,128)(2,1)S(1)}, u32[]{:S(2)}, u32[]{:S(2)}) %collective-permute-start.13) | collective-permute-done | bytes 2097184 | tf_op jit(solution)/shard_map/ppermute | solution.py:78
  315.1 25.8 %shard_map.219 = (bf16[2048,2048]{1,0:T(8,128)(2,1)}, bf16[2048,2048]{1,0:T(8,128)(2,1)}, bf16[2048,2048]{1,0:T(8,128)(2,1)}, bf16[2048,2048]{1,0:T(8,128)(2,1)}) custom-call(bf16[512,2048]{1,0:T(8,128)(2,1)} %copy-done.33, bf16[512,2048]{1,0:T(8,128)(2,1)} %copy-done.34, ...), custom_call_target="tpu_custom_call", output_to_operand_aliasing={{0}: (4, {}), {1}: (5, {}), {2}: (6, {}), {3}: (7, {})} | custom-call | flops 1073741824 | tf_op jit(solution)/shard_map/pallas_call | solution.py:374
  348.9 15.9 %shard_map.222 = (bf16[2048,2048]{1,0:T(8,128)(2,1)}, bf16[2048,2048]{1,0:T(8,128)(2,1)}, bf16[2048,2048]{1,0:T(8,128)(2,1)}, bf16[2048,2048]{1,0:T(8,128)(2,1)}) custom-call(bf16[512,2048]{1,0:T(8,128)(2,1)} %pad_maximum_fusion.1.refs_0_, ...), custom_call_target="tpu_custom_call", output_to_operand_aliasing={{0}: (3, {}), {1}: (4, {}), {2}: (5, {}), {3}: (6, {})} | custom-call | flops 536870912 | tf_op jit(solution)/shard_map/pallas_call | solution.py:374
  377.7 25.5 %shard_map.231.refs_0_ = bf16[2048,2048]{1,0:T(8,128)(2,1)} custom-call(bf16[512,2048]{1,0:T(8,128)(2,1)} %collective-permute-done.11.refs_2_.value_ref.refs_0_, bf16[512,2048]{1,0:T(8,128)(2,1)} %collective-permute-done.12.refs_3_.value_ref.refs_1_, bf16[512,2048]{1,0:T(8,128)(2,1)} %copy-done.30, bf16[512,2048]{1,0:T(8,128)(2,1)} %shard_map.212.refs_10_.refs_3_, ...), custom_call_target="tpu_custom_call" | custom-call | flops 1073741824 | tf_op jit(solution)/shard_map/pallas_call | solution.py:506
  405.4 19.3 %shard_map.225 = (bf16[512,2048]{1,0:T(8,128)(2,1)}, bf16[512,2048]{1,0:T(8,128)(2,1)}, bf16[512,2048]{1,0:T(8,128)(2,1)}) custom-call(s32[3]{0:T(128)S(1)} %copy-done.23, bf16[2048,2048]{1,0:T(8,128)(2,1)} %get-tuple-element.80.refs_0_.refs_2_.refs_1_.refs_4_, bf16[2048,2048]{1,0:T(8,128)(2,1)} %get-tuple-element.80.refs_0_.refs_2_.refs_1_.refs_4_, ...), custom_call_target="tpu_custom_call" | custom-call | flops 805306368 | tf_op jit(solution)/shard_map/pallas_call | solution.py:431
  428.5 27.1 %shard_map.226 = (bf16[2048,2048]{1,0:T(8,128)(2,1)}, bf16[2048,2048]{1,0:T(8,128)(2,1)}) custom-call(bf16[512,2048]{1,0:T(8,128)(2,1)} %collective-permute-done.11.refs_2_.value_ref.refs_0_, bf16[512,2048]{1,0:T(8,128)(2,1)} %collective-permute-done.12.refs_3_.value_ref.refs_1_, bf16[512,2048]{1,0:T(8,128)(2,1)} %copy-done.30, ...), custom_call_target="tpu_custom_call" | custom-call | flops 1073741824 | tf_op jit(solution)/shard_map/pallas_call | solution.py:374
  455.6 13.9 %shard_map.227 = (bf16[256,2048]{1,0:T(8,128)(2,1)S(1)}, bf16[256,2048]{1,0:T(8,128)(2,1)}) custom-call(s32[1]{0:T(128)} %constant.53.clone.1.slot_ref, bf16[2048,2048]{1,0:T(8,128)(2,1)} %get-tuple-element.93.refs_0_.refs_2_.refs_1_, bf16[2048,2048]{1,0:T(8,128)(2,1)} %get-tuple-element.94.refs_1_.refs_3_, ...), custom_call_target="tpu_custom_call" | custom-call | flops 536870912 | tf_op jit(solution)/shard_map/pallas_call | solution.py:431
  471.8 25.9 %shard_map.234.refs_0_ = bf16[2048,2048]{1,0:T(8,128)(2,1)} custom-call(bf16[2048,2048]{1,0:T(8,128)(2,1)} %get-tuple-element.103.refs_0_, bf16[2048,2048]{1,0:T(8,128)(2,1)} %get-tuple-element.93.refs_0_.refs_2_.refs_1_, bf16[256,2048]{1,0:T(8,128)(2,1)S(1)} %get-tuple-element.96.refs_2_, bf16[512,2048]{1,0:T(8,128)(2,1)} %copy-done.35, ...), custom_call_target="tpu_custom_call" | custom-call | flops 1073741824 | tf_op jit(solution)/shard_map/pallas_call | solution.py:506
  500.8 24.7 %shard_map.228 = (bf16[512,2048]{1,0:T(8,128)(2,1)}, bf16[512,2048]{1,0:T(8,128)(2,1)}) custom-call(s32[2]{0:T(128)S(1)} %iota.41.slot_ref, bf16[2048,2048]{1,0:T(8,128)(2,1)} %get-tuple-element.93.refs_0_.refs_2_.refs_1_, bf16[2048,2048]{1,0:T(8,128)(2,1)} %get-tuple-element.94.refs_1_.refs_3_, ...), custom_call_target="tpu_custom_call" | custom-call | flops 1073741824 | tf_op jit(solution)/shard_map/pallas_call | solution.py:431
  529.2 14.0 %shard_map.229.refs_0_.refs_2_ = bf16[512,2048]{1,0:T(8,128)(2,1)} custom-call(s32[1]{0:T(128)} %constant.61.clone.1.slot_ref, bf16[2048,2048]{1,0:T(8,128)(2,1)} %get-tuple-element.93.refs_0_.refs_2_.refs_1_, bf16[2048,2048]{1,0:T(8,128)(2,1)} %get-tuple-element.94.refs_1_.refs_3_, ...), custom_call_target="tpu_custom_call" | custom-call | flops 536870912 | tf_op jit(solution)/shard_map/pallas_call | solution.py:431
  543.3 25.8 %shard_map.247.refs_0_ = bf16[2048,2048]{1,0:T(8,128)(2,1)} custom-call(bf16[2048,2048]{1,0:T(8,128)(2,1)} %get-tuple-element.103.refs_0_, bf16[2048,2048]{1,0:T(8,128)(2,1)} %get-tuple-element.94.refs_1_.refs_3_, bf16[512,2048]{1,0:T(8,128)(2,1)} %shard_map.229.refs_0_.refs_2_), custom_call_target="tpu_custom_call" | custom-call | flops 1073741824 | tf_op jit(solution)/shard_map/pallas_call | solution.py:506
  571.2 13.8 %shard_map.230 = (f32[512,2048]{1,0:T(8,128)}, bf16[512,2048]{1,0:T(8,128)(2,1)}, bf16[512,512]{1,0:T(8,128)(2,1)S(1)}, bf16[512,512]{1,0:T(8,128)(2,1)S(1)}, bf...) custom-call(bf16[512,2048]{1,0:T(8,128)(2,1)} %shard_map.229.refs_0_.refs_2_, bf16[512,2048]{1,0:T(8,128)(2,1)} %copy-done.31, ...), custom_call_target="tpu_custom_call" | custom-call | flops 268435456 | tf_op jit(solution)/shard_map/pallas_call | solution.py:616
  611.9 18.7 %collective-permute-start.34 = (bf16[512,2048]{1,0:T(8,128)(2,1)}, bf16[512,2048]{1,0:T(8,128)(2,1)}, u32[]{:S(2)}, u32[]{:S(2)}) collective-permute-start(bf16[512,2048]{1,0:T(8,128)(2,1)} %shard_map.244.refs_3_), channel_id=1, source_target_pairs={{0,1},{1,0},{2,3},{3,2},{4,5},{5,4},{6,7},{7,6},{8,9},{9,8},{10,11... | collective-permute-start | bytes 6291464 | tf_op jit(solution)/shard_map/ppermute | solution.py:160
  633.0 72.2 %shard_map.233.refs_0_.refs_1_.refs_5_ = bf16[2048,768]{1,0:T(8,128)(2,1)} custom-call(s32[5]{0:T(128)S(1)} %stack.68.order_ref, bf16[2048,512]{1,0:T(8,128)(2,1)} %get-tuple-element.61.q_ref.rest_0_, bf16[2,2,2048,128]{3,2,1,0:T(8,128)(2,1)} %get-tuple-element.62.kx_ref, bf16[2,2,2048,128]{3,2,1,0:T(8,128)(2,1)} %get-tuple-element.87.vx_ref, ...), custom_call_target="tpu_custom_call" | custom-call | flops 6710886400 | tf_op jit(solution)/shard_map/pallas_call | solution.py:901
  720.9 17.0 %shard_map.245.refs_0_ = bf16[2048,1280]{1,0:T(8,128)(2,1)} custom-call(bf16[2048,2048]{1,0:T(8,128)(2,1)} %shard_map.243.refs_0_, bf16[512,2048]{1,0:T(8,128)(2,1)} %collective-permute-done.34.refs_1_, bf16[512,2048]{1,0:T(8,128)(2,1)} %collective-permute-done.35.refs_2_, bf16[512,2048]{1,0:T(8,128)(2,1)} %shard_map.244.refs_3_, ...), custom_call_target="tpu_custom_call" | custom-call | flops 671088640 | tf_op jit(solution)/shard_map/pallas_call | solution.py:537
  759.3 17.3 %collective-permute-done.37 = f32[1,2048]{1,0:T(1,128)S(1)} collective-permute-done((f32[1,2048]{1,0:T(1,128)S(1)}, f32[1,2048]{1,0:T(1,128)S(1)}, u32[]{:S(2)}, u32[]{:S(2)}) %collective-permute-start.37) | collective-permute-done | bytes 8224 | tf_op jit(solution)/shard_map/ppermute | solution.py:171
  799.6 29.2 %collective-permute-start.42 = (f32[1,2048]{1,0:T(1,128)S(1)}, f32[1,2048]{1,0:T(1,128)S(1)}, u32[]{:S(2)}, u32[]{:S(2)}) collective-permute-start(f32[1,2048]{1,0:T(1,128)S(1)} %add.61), channel_id=1, source_target_pairs={{0,16},{4,20},{8,24},{12,28},{16,0},{20,4},{24,8},{28,12},{1,17},{... | collective-permute-start | bytes 24584 | tf_op jit(solution)/shard_map/ppermute | solution.py:179
  (298 shorter events, 235.6 us)
Async XLA Ops:
  7.2 89.2 %all-gather.4.cloned.1.call-start = ((), (), s32[]{:S(2)}) async-start(), calls=%async_computation.4 | async-start | bytes 7077888 | tf_op jit(solution)/shard_map/all_gather | solution.py:942
  13.6 239.4 %all-gather.6.cloned.1.call-start = ((), (), s32[]{:S(2)}) async-start(), calls=%async_computation.5 | async-start | bytes 18874368 | tf_op jit(solution)/shard_map/all_gather | solution.py:948
  13.7 48.6 %collective-permute-start = (bf16[512,2048]{1,0:T(8,128)(2,1)S(1)}, bf16[512,2048]{1,0:T(8,128)(2,1)S(1)}, u32[]{:S(2)}, u32[]{:S(2)}) collective-permute-start(bf16[512,2048]{1,0:T(8,128)(2,1)S(1)} %copy-done.27), channel_id=1, source_target_pairs={{0,1},{1,0},{2,3},{3,2},{4,5},{5,4},{6,7},{7,6},{8,9},{9,8},{10,11... | collective-permute-start | bytes 6291464 | tf_op jit(solution)/shard_map/ppermute | solution.py:78
  16.7 47.2 %collective-permute-start.1 = (bf16[512,2048]{1,0:T(8,128)(2,1)S(1)}, bf16[512,2048]{1,0:T(8,128)(2,1)}, u32[]{:S(2)}, u32[]{:S(2)}) collective-permute-start(bf16[512,2048]{1,0:T(8,128)(2,1)S(1)} %copy-done.27), channel_id=1, source_target_pairs={{0,2},{1,3},{2,0},{3,1},{4,6},{5,7},{6,4},{7,5},{8,10},{9,11},{10,... | collective-permute-start | bytes 6291464 | tf_op jit(solution)/shard_map/ppermute | solution.py:78
  63.9 300.9 %all-gather.8.cloned.1.call-start = ((), (), s32[]{:S(2)}) async-start(), calls=%async_computation.6 | async-start | bytes 9437184 | tf_op jit(solution)/shard_map/all_gather | solution.py:957
  100.3 54.2 %collective-permute-start.5 = (bf16[2048,512]{1,0:T(8,128)(2,1)}, bf16[2048,512]{1,0:T(8,128)(2,1)}, u32[]{:S(2)}, u32[]{:S(2)}) collective-permute-start(bf16[2048,512]{1,0:T(8,128)(2,1)} %shard_map.206.refs_4_.refs_3_), channel_id=1, source_target_pairs={{0,2},{1,3},{2,0},{3,1},{4,6},{5,7},{6,4},{7,5},{8,10},{9,11},{10,... | collective-permute-start | bytes 6291464 | tf_op jit(solution)/shard_map/ppermute | solution.py:78
  100.8 56.3 %collective-permute-start.4 = (bf16[2048,512]{1,0:T(8,128)(2,1)}, bf16[2048,512]{1,0:T(8,128)(2,1)}, u32[]{:S(2)}, u32[]{:S(2)}) collective-permute-start(bf16[2048,512]{1,0:T(8,128)(2,1)} %shard_map.206.refs_4_.refs_3_), channel_id=1, source_target_pairs={{0,1},{1,0},{2,3},{3,2},{4,5},{5,4},{6,7},{7,6},{8,9},{9,8},{10,11... | collective-permute-start | bytes 6291464 | tf_op jit(solution)/shard_map/ppermute | solution.py:78
  125.8 507.2 %reduce-scatter.5.cloned.1.call-start = ((), (), s32[]{:S(2)}) async-start(), calls=%async_computation.7 | async-start | bytes 9437184 | tf_op jit(solution)/shard_map/reduce_scatter | solution.py:1005
  185.8 83.0 %collective-permute-start.11 = (bf16[512,2048]{1,0:T(8,128)(2,1)}, bf16[512,2048]{1,0:T(8,128)(2,1)}, u32[]{:S(2)}, u32[]{:S(2)}) collective-permute-start(bf16[512,2048]{1,0:T(8,128)(2,1)} %shard_map.212.refs_10_.refs_3_), channel_id=1, source_target_pairs={{0,1},{1,0},{2,3},{3,2},{4,5},{5,4},{6,7},{7,6},{8,9},{9,8},{10,11... | collective-permute-start | bytes 6291464 | tf_op jit(solution)/shard_map/ppermute | solution.py:78
  187.3 81.5 %collective-permute-start.12 = (bf16[512,2048]{1,0:T(8,128)(2,1)}, bf16[512,2048]{1,0:T(8,128)(2,1)}, u32[]{:S(2)}, u32[]{:S(2)}) collective-permute-start(bf16[512,2048]{1,0:T(8,128)(2,1)} %shard_map.212.refs_10_.refs_3_), channel_id=1, source_target_pairs={{0,2},{1,3},{2,0},{3,1},{4,6},{5,7},{6,4},{7,5},{8,10},{9,11},{10,... | collective-permute-start | bytes 6291464 | tf_op jit(solution)/shard_map/ppermute | solution.py:78
  187.8 45.5 %collective-permute-start.6 = (bf16[512,512]{1,0:T(8,128)(2,1)S(1)}, bf16[512,512]{1,0:T(8,128)(2,1)S(1)}, u32[]{:S(2)}, u32[]{:S(2)}) collective-permute-start(bf16[512,512]{1,0:T(8,128)(2,1)S(1)} %copy-done.15), channel_id=1, source_target_pairs={{0,1},{1,0},{2,3},{3,2},{4,5},{5,4},{6,7},{7,6},{8,9},{9,8},{10,11... | collective-permute-start | bytes 1572872 | tf_op jit(solution)/shard_map/ppermute | solution.py:968
  188.5 53.2 %collective-permute-start.7 = (bf16[512,512]{1,0:T(8,128)(2,1)S(1)}, bf16[512,512]{1,0:T(8,128)(2,1)S(1)}, u32[]{:S(2)}, u32[]{:S(2)}) collective-permute-start(bf16[512,512]{1,0:T(8,128)(2,1)S(1)} %get-tuple-element.68), channel_id=1, source_target_pairs={{0,2},{1,3},{2,0},{3,1},{4,6},{5,7},{6,4},{7,5},{8,10},{9,11},{10,... | collective-permute-start | bytes 1572872 | tf_op jit(solution)/shard_map/ppermute | solution.py:969
  189.9 51.8 %collective-permute-start.8 = (bf16[512,512]{1,0:T(8,128)(2,1)S(1)}, bf16[512,512]{1,0:T(8,128)(2,1)S(1)}, u32[]{:S(2)}, u32[]{:S(2)}) collective-permute-start(bf16[512,512]{1,0:T(8,128)(2,1)S(1)} %get-tuple-element.69), channel_id=1, source_target_pairs={{0,3},{1,2},{2,1},{3,0},{4,7},{5,6},{6,5},{7,4},{8,11},{9,10},{10,... | collective-permute-start | bytes 1572872 | tf_op jit(solution)/shard_map/ppermute | solution.py:970
  404.2 301.0 %reduce-scatter.7.cloned.1.call-start = ((), (), s32[]{:S(2)}) async-start(), calls=%async_computation.8 | async-start | bytes 9437184 | tf_op jit(solution)/shard_map/reduce_scatter | solution.py:1005
  424.7 45.0 %collective-permute-start.19 = (bf16[512,2048]{1,0:T(8,128)(2,1)}, bf16[512,2048]{1,0:T(8,128)(2,1)S(1)}, u32[]{:S(2)}, u32[]{:S(2)}) collective-permute-start(bf16[512,2048]{1,0:T(8,128)(2,1)} %get-tuple-element.84.refs_7_), channel_id=1, source_target_pairs={{0,1},{1,0},{2,3},{3,2},{4,5},{5,4},{6,7},{7,6},{8,9},{9,8},{10,11... | collective-permute-start | bytes 6291464 | tf_op jit(solution)/shard_map/ppermute | solution.py:1038
  426.5 43.2 %collective-permute-start.20 = (bf16[512,2048]{1,0:T(8,128)(2,1)}, bf16[512,2048]{1,0:T(8,128)(2,1)S(1)}, u32[]{:S(2)}, u32[]{:S(2)}) collective-permute-start(bf16[512,2048]{1,0:T(8,128)(2,1)} %get-tuple-element.85), channel_id=1, source_target_pairs={{0,2},{1,3},{2,0},{3,1},{4,6},{5,7},{6,4},{7,5},{8,10},{9,11},{10,... | collective-permute-start | bytes 6291464 | tf_op jit(solution)/shard_map/ppermute | solution.py:1039
  499.6 277.6 %reduce-scatter.11.cloned.1.call-start = ((), (), s32[]{:S(2)}) async-start(), calls=%async_computation.10 | async-start | bytes 9437184 | tf_op jit(solution)/shard_map/reduce_scatter | solution.py:1005
  525.6 43.5 %collective-permute-start.25 = (bf16[512,2048]{1,0:T(8,128)(2,1)}, bf16[512,2048]{1,0:T(8,128)(2,1)S(1)}, u32[]{:S(2)}, u32[]{:S(2)}) collective-permute-start(bf16[512,2048]{1,0:T(8,128)(2,1)} %get-tuple-element.97.refs_4_), channel_id=1, source_target_pairs={{0,1},{1,0},{2,3},{3,2},{4,5},{5,4},{6,7},{7,6},{8,9},{9,8},{10,11... | collective-permute-start | bytes 6291464 | tf_op jit(solution)/shard_map/ppermute | solution.py:1050
  570.4 269.5 %reduce-scatter.9.cloned.1.call-start = ((), (), s32[]{:S(2)}) async-start(), calls=%async_computation.9 | async-start | bytes 5898240 | tf_op jit(solution)/shard_map/reduce_scatter | solution.py:1005
  611.9 109.0 %collective-permute-start.34 = (bf16[512,2048]{1,0:T(8,128)(2,1)}, bf16[512,2048]{1,0:T(8,128)(2,1)}, u32[]{:S(2)}, u32[]{:S(2)}) collective-permute-start(bf16[512,2048]{1,0:T(8,128)(2,1)} %shard_map.244.refs_3_), channel_id=1, source_target_pairs={{0,1},{1,0},{2,3},{3,2},{4,5},{5,4},{6,7},{7,6},{8,9},{9,8},{10,11... | collective-permute-start | bytes 6291464 | tf_op jit(solution)/shard_map/ppermute | solution.py:160
  630.6 90.3 %collective-permute-start.35 = (bf16[512,2048]{1,0:T(8,128)(2,1)}, bf16[512,2048]{1,0:T(8,128)(2,1)}, u32[]{:S(2)}, u32[]{:S(2)}) collective-permute-start(bf16[512,2048]{1,0:T(8,128)(2,1)} %shard_map.244.refs_3_), channel_id=1, source_target_pairs={{0,2},{1,3},{2,0},{3,1},{4,6},{5,7},{6,4},{7,5},{8,10},{9,11},{10,... | collective-permute-start | bytes 6291464 | tf_op jit(solution)/shard_map/ppermute | solution.py:160
  631.6 89.4 %collective-permute-start.36 = (bf16[512,2048]{1,0:T(8,128)(2,1)}, bf16[512,2048]{1,0:T(8,128)(2,1)}, u32[]{:S(2)}, u32[]{:S(2)}) collective-permute-start(bf16[512,2048]{1,0:T(8,128)(2,1)} %shard_map.244.refs_3_), channel_id=1, source_target_pairs={{0,3},{1,2},{2,1},{3,0},{4,7},{5,6},{6,5},{7,4},{8,11},{9,10},{10,... | collective-permute-start | bytes 6291464 | tf_op jit(solution)/shard_map/ppermute | solution.py:160
  746.1 84.9 %collective-permute-start.33 = (bf16[512,2048]{1,0:T(8,128)(2,1)}, bf16[512,2048]{1,0:T(8,128)(2,1)S(1)}, u32[]{:S(2)}, u32[]{:S(2)}) collective-permute-start(bf16[512,2048]{1,0:T(8,128)(2,1)} %shard_map.239.refs_3_), channel_id=1, source_target_pairs={{0,2},{1,3},{2,0},{3,1},{4,6},{5,7},{6,4},{7,5},{8,10},{9,11},{10,... | collective-permute-start | bytes 6291464 | tf_op jit(solution)/shard_map/ppermute | solution.py:1099
  750.2 80.8 %collective-permute-start.32 = (bf16[512,2048]{1,0:T(8,128)(2,1)}, bf16[512,2048]{1,0:T(8,128)(2,1)}, u32[]{:S(2)}, u32[]{:S(2)}) collective-permute-start(bf16[512,2048]{1,0:T(8,128)(2,1)} %shard_map.238.refs_2_), channel_id=1, source_target_pairs={{0,1},{1,0},{2,3},{3,2},{4,5},{5,4},{6,7},{7,6},{8,9},{9,8},{10,11... | collective-permute-start | bytes 6291464 | tf_op jit(solution)/shard_map/ppermute | solution.py:1098
  (80 other events, 1251.1 us)
Sparse Core Ops, SparseCore 0:
  13.7 67.4 all-gather.3
  82.8 149.7 all-gather.5
  234.2 80.2 all-gather.7
  404.4 103.0 reduce-scatter.4
  509.6 97.5 reduce-scatter.6
  609.3 87.9 reduce-scatter.10
  740.1 67.4 reduce-scatter.8
